TPU v7x, 32 devices: a whole 2x2x4 slice. The times are simulated.
32 devices in a mesh: ctx: 16 (over z, x, core), fsdp: 2 (over y).
Axes of the slice: x: 2, y: 2, z: 4, core: 2. Of those that a mesh axis runs over, the one named last changes fastest.
Arguments:
- tokens: bfloat16 [4096, 1152], P(('ctx', 'fsdp')), may hold values from -6 to 6
- query_weight: bfloat16 [1152, 1152], P('fsdp'), may hold values from -0.4375 to 0.4375
- key_projection: bfloat16 [1152, 384], P('fsdp'), may hold values from -0.1875 to 0.1875
- value_projection: bfloat16 [1152, 384], P('fsdp'), may hold values from -0.1875 to 0.1875
- output_weight: bfloat16 [1152, 1152], P('fsdp'), may hold values from -1 to 1
- gate_weight: bfloat16 [1152, 3072], P('fsdp'), may hold values from -0.1875 to 0.1875
- up_weight: bfloat16 [1152, 3072], P('fsdp'), may hold values from -0.1875 to 0.1875
- down_weight: bfloat16 [3072, 1152], P('fsdp'), may hold values from -0.109375 to 0.109375
- norm_attn: bfloat16 [1152], P('fsdp'), may hold values from 0.5 to 1.5
- norm_mlp: bfloat16 [1152], P('fsdp'), may hold values from 0.5 to 1.5
- doc_starts: int32 [4], replicated, may hold values from 0 to 4095, as said below
- cotangent: bfloat16 [4096, 1152], P(('ctx', 'fsdp')), may hold values from -6 to 6
Outputs:
- result: bfloat16 [4096, 1152], P(('ctx', 'fsdp'))
- tokens_grad: float32 [4096, 1152], P(('ctx', 'fsdp'))
- query_grad: float32 [1152, 1152], P('fsdp', 'ctx')
- key_grad: float32 [1152, 384], P('fsdp', 'ctx')
- value_grad: float32 [1152, 384], P('fsdp', 'ctx')
- output_grad: float32 [1152, 1152], P('fsdp', 'ctx')
- gate_grad: float32 [1152, 3072], P('fsdp', 'ctx')
- up_grad: float32 [1152, 3072], P('fsdp', 'ctx')
- down_grad: float32 [3072, 1152], P('fsdp', 'ctx')
- norm_attn_grad: float32 [1152], replicated
- norm_mlp_grad: float32 [1152], replicated
Inputs may be any that keep to these rules, and one draw needn't show every extreme that they name: `doc_starts`: strictly increasing positions where documents begin, the first 0 and the last 4095; the second is one of positions 1 to 64 and the third one of positions 4032 to 4094, so one document runs from the first device's tokens to the last device's.
All inputs are finite; a program needn't handle non-finite values.
Results may differ from a plain program's by a relative error of at most 0.02.
Values may be sent and summed in bfloat16 or wider, within the bound.
A program may use at most 384 MiB of HBM per device.

v0:
```python
import math

import jax
import jax.numpy as jnp
from jax import lax
from jax.sharding import PartitionSpec as P

QUERY_HEADS = 18
KEY_VALUE_HEADS = 6
HEAD_SIZE = 64


EPS = 1e-05
THETA = 10000.0


def rope_tables(positions):
    half_dim = HEAD_SIZE // 2
    frequency = jnp.exp(-math.log(THETA) * jnp.arange(half_dim, dtype=jnp.float32) / half_dim)
    angles = positions.astype(jnp.float32)[:, None] * frequency[None, :]
    return (jnp.cos(angles), jnp.sin(angles))


def apply_rotary(values, cosine_table, sine_table):
    half_dim = values.shape[-1] // 2
    first_half = values[..., :half_dim]
    second_half = values[..., half_dim:]
    cos_rows = cosine_table[:, None, :]
    sin_rows = sine_table[:, None, :]
    return jnp.concatenate(
        [
            first_half * cos_rows - second_half * sin_rows,
            second_half * cos_rows + first_half * sin_rows,
        ],
        axis=-1,
    )


def unrotate(values, cosine_table, sine_table):
    half_dim = values.shape[-1] // 2
    first_half = values[..., :half_dim]
    second_half = values[..., half_dim:]
    cos_rows = cosine_table[:, None, :]
    sin_rows = sine_table[:, None, :]
    return jnp.concatenate(
        [
            first_half * cos_rows + second_half * sin_rows,
            second_half * cos_rows - first_half * sin_rows,
        ],
        axis=-1,
    )


def doc_begin(indices, doc_starts):
    marked = jnp.where(indices[:, None] >= doc_starts[None, :], doc_starts[None, :], 0)
    return jnp.max(marked, axis=1)


def layout_rows(device, row_count):
    return device * row_count + jnp.arange(row_count, dtype=jnp.int32)


def block_scores(query_rows, key_row_matrix, key_first, query_index, query_begin):
    scores = jnp.einsum(
        "rgjd,kgd->gjrk", query_rows, key_row_matrix, preferred_element_type=jnp.float32
    ) * (1.0 / math.sqrt(HEAD_SIZE))
    key_index = key_first + jnp.arange(key_row_matrix.shape[0], dtype=jnp.int32)
    allowed = (key_index[None, :] <= query_index[:, None]) & (
        key_index[None, :] >= query_begin[:, None]
    )
    return (scores, allowed[None, None])


def touches(key_first, row_count, query_index, query_begin):
    return (key_first <= jnp.max(query_index)) & (key_first + row_count - 1 >= jnp.min(query_begin))


def forward_step(query_rows, query_index, query_begin, carried, fragment):
    head_groups = query_rows.shape[1]
    key_all, value_all = fragment
    overall_rows = key_all.shape[0]
    rows_per_block = math.gcd(overall_rows, 512)

    def forward_block_step(turn_index, running):
        first_row = turn_index * rows_per_block
        key_row_matrix = lax.dynamic_slice_in_dim(key_all, first_row, rows_per_block, 0).reshape(
            rows_per_block, head_groups, HEAD_SIZE
        )
        value_row_matrix = lax.dynamic_slice_in_dim(
            value_all, first_row, rows_per_block, 0
        ).reshape(rows_per_block, head_groups, HEAD_SIZE)

        def forward_update(running):
            run_max, run_sum, accumulated = running
            scores, allowed = block_scores(
                query_rows, key_row_matrix, first_row, query_index, query_begin
            )
            scores = jnp.where(allowed, scores, -jnp.inf)
            new_max = jnp.maximum(run_max, jnp.max(scores, axis=-1))
            safe_max = jnp.where(new_max == -jnp.inf, 0.0, new_max)
            weights = jnp.exp(scores - safe_max[..., None])
            decay_factor = jnp.exp(run_max - safe_max)
            run_sum = run_sum * decay_factor + jnp.sum(weights, axis=-1)
            accumulated = accumulated * decay_factor[..., None] + jnp.einsum(
                "gjrk,kgd->gjrd",
                weights.astype(jnp.bfloat16),
                value_row_matrix,
                preferred_element_type=jnp.float32,
            )
            return (new_max, run_sum, accumulated)

        def forward_unchanged(running):
            return running

        return lax.cond(
            touches(first_row, rows_per_block, query_index, query_begin),
            forward_update,
            forward_unchanged,
            running,
        )

    return lax.fori_loop(0, overall_rows // rows_per_block, forward_block_step, carried)


def backward_probs(
    query_rows,
    grads_out,
    log_total,
    row_delta,
    key_row_matrix,
    value_row_matrix,
    key_first,
    query_index,
    query_begin,
):
    scores, allowed = block_scores(query_rows, key_row_matrix, key_first, query_index, query_begin)
    probabilities = jnp.exp(jnp.where(allowed, scores - log_total[..., None], -jnp.inf))
    grad_prob = jnp.einsum(
        "rgjd,kgd->gjrk", grads_out, value_row_matrix, preferred_element_type=jnp.float32
    )
    grad_score = (probabilities * (grad_prob - row_delta[..., None])).astype(jnp.bfloat16)
    return (probabilities, grad_score)


def query_grads(
    query_rows, grads_out, log_total, row_delta, query_index, query_begin, key_all, value_all
):
    head_groups = query_rows.shape[1]
    overall_rows = key_all.shape[0]
    rows_per_block = math.gcd(overall_rows, 512)
    start_grad = jnp.zeros(
        (head_groups, query_rows.shape[2], query_rows.shape[0], HEAD_SIZE), jnp.float32
    )

    def query_block_step(turn_index, accumulated):
        key_first = turn_index * rows_per_block
        key_row_matrix = lax.dynamic_slice_in_dim(key_all, key_first, rows_per_block, 0).reshape(
            rows_per_block, head_groups, HEAD_SIZE
        )
        value_row_matrix = lax.dynamic_slice_in_dim(
            value_all, key_first, rows_per_block, 0
        ).reshape(rows_per_block, head_groups, HEAD_SIZE)

        def query_update(accumulated):
            probabilities, grad_score = backward_probs(
                query_rows,
                grads_out,
                log_total,
                row_delta,
                key_row_matrix,
                value_row_matrix,
                key_first,
                query_index,
                query_begin,
            )
            return accumulated + jnp.einsum(
                "gjrk,kgd->gjrd", grad_score, key_row_matrix, preferred_element_type=jnp.float32
            ) * (1.0 / math.sqrt(HEAD_SIZE))

        def query_unchanged(accumulated):
            return accumulated

        return lax.cond(
            touches(key_first, rows_per_block, query_index, query_begin),
            query_update,
            query_unchanged,
            accumulated,
        )

    return lax.fori_loop(0, overall_rows // rows_per_block, query_block_step, start_grad)


def key_grads(
    query_rows,
    grads_out,
    log_total,
    row_delta,
    query_index,
    query_begin,
    key_all,
    value_all,
    row_count,
):
    head_groups = query_rows.shape[1]
    row_width = head_groups * HEAD_SIZE
    rows_per_block = math.gcd(row_count, 512)

    def block_term(turn_index):
        key_first = turn_index * rows_per_block
        key_row_matrix = lax.dynamic_slice_in_dim(key_all, key_first, rows_per_block, 0).reshape(
            rows_per_block, head_groups, HEAD_SIZE
        )
        value_row_matrix = lax.dynamic_slice_in_dim(
            value_all, key_first, rows_per_block, 0
        ).reshape(rows_per_block, head_groups, HEAD_SIZE)

        def compute(operand):
            probabilities, grad_score = backward_probs(
                query_rows,
                grads_out,
                log_total,
                row_delta,
                key_row_matrix,
                value_row_matrix,
                key_first,
                query_index,
                query_begin,
            )
            grad_value = jnp.einsum(
                "gjrk,rgjd->kgd",
                probabilities.astype(jnp.bfloat16),
                grads_out,
                preferred_element_type=jnp.float32,
            )
            grad_key = jnp.einsum(
                "gjrk,rgjd->kgd", grad_score, query_rows, preferred_element_type=jnp.float32
            ) * (1.0 / math.sqrt(HEAD_SIZE))
            return jnp.concatenate(
                [
                    grad_key.reshape(rows_per_block, row_width),
                    grad_value.reshape(rows_per_block, row_width),
                ],
                axis=1,
            )

        def nothing(operand):
            return jnp.zeros((rows_per_block, 2 * row_width), jnp.float32)

        return lax.cond(
            touches(key_first, rows_per_block, query_index, query_begin), compute, nothing, 0
        )

    blocks = lax.map(block_term, jnp.arange(row_count // rows_per_block, dtype=jnp.int32))
    return blocks.reshape(row_count, 2 * row_width)


def per_device(
    tokens,
    query_weight,
    key_projection,
    value_projection,
    output_weight,
    gate_weight,
    up_weight,
    down_weight,
    norm_attn,
    norm_mlp,
    doc_starts,
    cotangent,
):
    (
        query_full,
        key_full,
        value_full,
        output_full,
        gate_full,
        up_full,
        down_full,
        gain_attn,
        gain_mlp,
    ) = (
        lax.all_gather(query_weight, "fsdp", axis=0, tiled=True),
        lax.all_gather(key_projection, "fsdp", axis=0, tiled=True),
        lax.all_gather(value_projection, "fsdp", axis=0, tiled=True),
        lax.all_gather(output_weight, "fsdp", axis=0, tiled=True),
        lax.all_gather(gate_weight, "fsdp", axis=0, tiled=True),
        lax.all_gather(up_weight, "fsdp", axis=0, tiled=True),
        lax.all_gather(down_weight, "fsdp", axis=0, tiled=True),
        lax.all_gather(norm_attn, "fsdp", axis=0, tiled=True),
        lax.all_gather(norm_mlp, "fsdp", axis=0, tiled=True),
    )
    token_rows = tokens.shape[0]
    head_groups = KEY_VALUE_HEADS
    queries_per_group = QUERY_HEADS // KEY_VALUE_HEADS
    gain_attn = gain_attn.astype(jnp.float32)
    gain_mlp = gain_mlp.astype(jnp.float32)
    hidden = tokens.astype(jnp.float32)
    inv_attn = lax.rsqrt(jnp.mean(hidden * hidden, axis=-1, keepdims=True) + EPS)
    normed_attn = hidden * inv_attn
    attention_input = (normed_attn * gain_attn).astype(jnp.bfloat16)
    own_device = lax.axis_index(("ctx", "fsdp"))
    own_index = layout_rows(own_device, token_rows)
    own_begin = doc_begin(own_index, doc_starts)
    cosine_table, sine_table = rope_tables(own_index - own_begin)
    query_pre = jnp.dot(attention_input, query_full, preferred_element_type=jnp.float32).reshape(
        token_rows, QUERY_HEADS, HEAD_SIZE
    )
    key_unrotated = jnp.dot(attention_input, key_full, preferred_element_type=jnp.float32).reshape(
        token_rows, KEY_VALUE_HEADS, HEAD_SIZE
    )
    query_rot = (
        apply_rotary(query_pre, cosine_table, sine_table)
        .astype(jnp.bfloat16)
        .reshape(token_rows, QUERY_HEADS * HEAD_SIZE)
    )
    key_rotated = (
        apply_rotary(key_unrotated, cosine_table, sine_table)
        .astype(jnp.bfloat16)
        .reshape(token_rows, KEY_VALUE_HEADS * HEAD_SIZE)
    )
    value_reduced = jnp.dot(attention_input, value_full, preferred_element_type=jnp.float32).astype(
        jnp.bfloat16
    )
    local_index = layout_rows(own_device, token_rows)
    local_begin = doc_begin(local_index, doc_starts)
    local_cos, local_sin = rope_tables(local_index - local_begin)
    query_rows = query_rot.reshape(token_rows, head_groups, queries_per_group, HEAD_SIZE)
    start_state = (
        jnp.full((head_groups, queries_per_group, token_rows), -jnp.inf, jnp.float32),
        jnp.zeros((head_groups, queries_per_group, token_rows), jnp.float32),
        jnp.zeros((head_groups, queries_per_group, token_rows, HEAD_SIZE), jnp.float32),
    )
    run_max, run_sum, accumulated = forward_step(
        query_rows,
        local_index,
        local_begin,
        start_state,
        (
            lax.all_gather(key_rotated, ("ctx", "fsdp"), axis=0, tiled=True),
            lax.all_gather(value_reduced, ("ctx", "fsdp"), axis=0, tiled=True),
        ),
    )
    attn_exact = accumulated / run_sum[..., None]
    log_total = run_max + jnp.log(run_sum)
    attn_local = (
        attn_exact.transpose(2, 0, 1, 3)
        .reshape(token_rows, QUERY_HEADS * HEAD_SIZE)
        .astype(jnp.bfloat16)
    )
    resid = hidden + jnp.dot(attn_local, output_full, preferred_element_type=jnp.float32)
    inv_mlp = lax.rsqrt(jnp.mean(resid * resid, axis=-1, keepdims=True) + EPS)
    normed_mlp = resid * inv_mlp
    mlp_in = (normed_mlp * gain_mlp).astype(jnp.bfloat16)
    gate_pre = jnp.dot(mlp_in, gate_full, preferred_element_type=jnp.float32)
    up_pre = jnp.dot(mlp_in, up_full, preferred_element_type=jnp.float32)
    gate_act = jax.nn.silu(gate_pre)
    mixed = (gate_act * up_pre).astype(jnp.bfloat16)
    result = (resid + jnp.dot(mixed, down_full, preferred_element_type=jnp.float32)).astype(
        jnp.bfloat16
    )
    down_partial = jnp.einsum("tf,td->fd", mixed, cotangent, preferred_element_type=jnp.float32)
    grad_mixed = jnp.einsum("td,fd->tf", cotangent, down_full, preferred_element_type=jnp.float32)
    sigmoid_gate = jax.nn.sigmoid(gate_pre)
    grad_gate = (
        grad_mixed * up_pre * sigmoid_gate * (1.0 + gate_pre * (1.0 - sigmoid_gate))
    ).astype(jnp.bfloat16)
    grad_up = (grad_mixed * gate_act).astype(jnp.bfloat16)
    gate_partial = jnp.einsum("td,tf->df", mlp_in, grad_gate, preferred_element_type=jnp.float32)
    up_partial = jnp.einsum("td,tf->df", mlp_in, grad_up, preferred_element_type=jnp.float32)
    grad_mlp_in = jnp.einsum(
        "tf,df->td", grad_gate, gate_full, preferred_element_type=jnp.float32
    ) + jnp.einsum("tf,df->td", grad_up, up_full, preferred_element_type=jnp.float32)
    gain_mlp_partial = jnp.sum(grad_mlp_in * normed_mlp, axis=0)
    scaled_mlp = grad_mlp_in * gain_mlp
    grad_resid = cotangent.astype(jnp.float32) + inv_mlp * (
        scaled_mlp - normed_mlp * jnp.mean(scaled_mlp * normed_mlp, axis=-1, keepdims=True)
    )
    grad_branch = grad_resid.astype(jnp.bfloat16)
    output_partial = jnp.einsum(
        "th,td->hd", attn_local, grad_branch, preferred_element_type=jnp.float32
    )
    grad_attn = jnp.einsum(
        "td,hd->th", grad_branch, output_full, preferred_element_type=jnp.float32
    ).astype(jnp.bfloat16)
    grads_out = grad_attn.reshape(token_rows, head_groups, queries_per_group, HEAD_SIZE)
    row_delta = jnp.sum(grads_out.astype(jnp.float32).transpose(1, 2, 0, 3) * attn_exact, axis=-1)
    key_all, value_all = (
        lax.all_gather(key_rotated, ("ctx", "fsdp"), axis=0, tiled=True),
        lax.all_gather(value_reduced, ("ctx", "fsdp"), axis=0, tiled=True),
    )
    grad_query_rot = query_grads(
        query_rows, grads_out, log_total, row_delta, local_index, local_begin, key_all, value_all
    )
    grad_kv = lax.psum_scatter(
        key_grads(
            query_rows,
            grads_out,
            log_total,
            row_delta,
            local_index,
            local_begin,
            key_all,
            value_all,
            token_rows * lax.axis_size(("ctx", "fsdp")),
        ),
        ("ctx", "fsdp"),
        scatter_dimension=0,
        tiled=True,
    )
    grad_query_local = (
        unrotate(
            grad_query_rot.transpose(2, 0, 1, 3).reshape(token_rows, QUERY_HEADS, HEAD_SIZE),
            local_cos,
            local_sin,
        )
        .astype(jnp.bfloat16)
        .reshape(token_rows, QUERY_HEADS * HEAD_SIZE)
    )
    grad_key = (
        unrotate(
            grad_kv[:, : head_groups * HEAD_SIZE].reshape(token_rows, head_groups, HEAD_SIZE),
            cosine_table,
            sine_table,
        )
        .astype(jnp.bfloat16)
        .reshape(token_rows, KEY_VALUE_HEADS * HEAD_SIZE)
    )
    grad_value = grad_kv[:, head_groups * HEAD_SIZE :].astype(jnp.bfloat16)
    query_partial = jnp.einsum(
        "td,th->dh", attention_input, grad_query_local, preferred_element_type=jnp.float32
    )
    key_partial = jnp.einsum(
        "td,th->dh", attention_input, grad_key, preferred_element_type=jnp.float32
    )
    value_partial = jnp.einsum(
        "td,th->dh", attention_input, grad_value, preferred_element_type=jnp.float32
    )
    grad_attn_in = jnp.einsum(
        "th,dh->td", grad_query_local, query_full, preferred_element_type=jnp.float32
    )
    grad_attn_in = grad_attn_in + jnp.einsum(
        "th,dh->td", grad_key, key_full, preferred_element_type=jnp.float32
    )
    grad_attn_in = grad_attn_in + jnp.einsum(
        "th,dh->td", grad_value, value_full, preferred_element_type=jnp.float32
    )
    gain_attn_partial = jnp.sum(grad_attn_in * normed_attn, axis=0)
    scaled_attn = grad_attn_in * gain_attn
    tokens_grad = grad_resid + inv_attn * (
        scaled_attn - normed_attn * jnp.mean(scaled_attn * normed_attn, axis=-1, keepdims=True)
    )
    query_pair, key_pair, value_pair, output_pair, gate_pair, up_pair, down_pair = (
        lax.psum_scatter(
            query_partial.astype(jnp.bfloat16), "fsdp", scatter_dimension=0, tiled=True
        ).astype(jnp.float32),
        lax.psum_scatter(
            key_partial.astype(jnp.bfloat16), "fsdp", scatter_dimension=0, tiled=True
        ).astype(jnp.float32),
        lax.psum_scatter(
            value_partial.astype(jnp.bfloat16), "fsdp", scatter_dimension=0, tiled=True
        ).astype(jnp.float32),
        lax.psum_scatter(
            output_partial.astype(jnp.bfloat16), "fsdp", scatter_dimension=0, tiled=True
        ).astype(jnp.float32),
        lax.psum_scatter(
            gate_partial.astype(jnp.bfloat16), "fsdp", scatter_dimension=0, tiled=True
        ).astype(jnp.float32),
        lax.psum_scatter(
            up_partial.astype(jnp.bfloat16), "fsdp", scatter_dimension=0, tiled=True
        ).astype(jnp.float32),
        lax.psum_scatter(
            down_partial.astype(jnp.bfloat16), "fsdp", scatter_dimension=0, tiled=True
        ).astype(jnp.float32),
    )
    query_sum, key_sum, value_sum, output_sum, gate_sum, up_sum, down_sum = (
        lax.psum_scatter(query_pair, "ctx", scatter_dimension=1, tiled=True),
        lax.psum_scatter(key_pair, "ctx", scatter_dimension=1, tiled=True),
        lax.psum_scatter(value_pair, "ctx", scatter_dimension=1, tiled=True),
        lax.psum_scatter(output_pair, "ctx", scatter_dimension=1, tiled=True),
        lax.psum_scatter(gate_pair, "ctx", scatter_dimension=1, tiled=True),
        lax.psum_scatter(up_pair, "ctx", scatter_dimension=1, tiled=True),
        lax.psum_scatter(down_pair, "ctx", scatter_dimension=1, tiled=True),
    )
    gain_attn_sum, gain_mlp_sum = lax.psum((gain_attn_partial, gain_mlp_partial), ("ctx", "fsdp"))
    return (
        result,
        tokens_grad,
        query_sum,
        key_sum,
        value_sum,
        output_sum,
        gate_sum,
        up_sum,
        down_sum,
        gain_attn_sum,
        gain_mlp_sum,
    )


def solution(mesh):
    return jax.shard_map(
        per_device,
        mesh=mesh,
        in_specs=(
            P(("ctx", "fsdp"), None),
            P("fsdp", None),
            P("fsdp", None),
            P("fsdp", None),
            P("fsdp", None),
            P("fsdp", None),
            P("fsdp", None),
            P("fsdp", None),
            P("fsdp"),
            P("fsdp"),
            P(),
            P(("ctx", "fsdp"), None),
        ),
        out_specs=(
            P(("ctx", "fsdp"), None),
            P(("ctx", "fsdp"), None),
            P("fsdp", "ctx"),
            P("fsdp", "ctx"),
            P("fsdp", "ctx"),
            P("fsdp", "ctx"),
            P("fsdp", "ctx"),
            P("fsdp", "ctx"),
            P("fsdp", "ctx"),
            P(),
            P(),
        ),
        check_vma=False,
    )
```

profile of v0, /device:TPU:15, one launch (start us, length us, event | category | flops | bytes accessed | tf_op | source)
XLA Modules:
  0.0 1536.9 jit_solution(1136647161189693912)
XLA Ops:
  16.6 20.4 %all_gather.39 = bf16[1152,384]{1,0:T(8,128)(2,1)S(1)} all-gather(bf16[576,384]{1,0:T(8,128)(2,1)} %param.27), channel_id=1, replica_groups=mesh['ctx'=16,'fsdp'=2] {'fsdp'}, dimensions={0}, use_global_device_ids=true | all-gather | bytes 1327104 | tf_op jit(solution)/shard_map/all_gather | solution.py:284
  40.8 21.1 %all_gather.36 = bf16[1152,384]{1,0:T(8,128)(2,1)S(1)} all-gather(bf16[576,384]{1,0:T(8,128)(2,1)S(1)} %copy-done.24), channel_id=1, replica_groups=mesh['ctx'=16,'fsdp'=2] {'fsdp'}, dimensions={0}, use_global_device_ids=true | all-gather | bytes 1327104 | tf_op jit(solution)/shard_map/all_gather | solution.py:283
  70.7 59.0 %all-gather.12.cloned.1.call-done = bf16[4096,384]{1,0:T(8,128)(2,1)} async-done(((bf16[128,384]{1,0:T(8,128)(2,1)}), bf16[4096,384]{1,0:T(8,128)(2,1)}) %all-gather.12.cloned.1.call-update) | async-done | bytes 3145744 | tf_op jit(solution)/shard_map/all_gather | solution.py:340
  129.8 4.8 copy.88
  134.6 56.6 %all-gather.8.cloned.1.call-done = bf16[4096,384]{0,1:T(8,128)(2,1)} async-done(((bf16[128,384]{0,1:T(8,128)(2,1)}), bf16[4096,384]{0,1:T(8,128)(2,1)}) %all-gather.8.cloned.1.call-update) | async-done | bytes 3145744 | tf_op jit(solution)/shard_map/all_gather | solution.py:339
  191.3 29.2 %while.58 = (s32[]{:T(128)}, f32[6,3,128]{2,1,0:T(4,128)S(1)}, f32[6,3,128]{2,1,0:T(4,128)S(1)}, f32[6,3,128,64]{2,3,1,0:T(8,128)S(1)}, s32[]{:T(128)}, /*index=...) while((s32[]{:T(128)}, f32[6,3,128]{2,1,0:T(4,128)S(1)}, ...), condition=%wide.region_9.10_spmd.clone, body=%wide.region_4.9_spmd.clone.sunk | while | flops 315472000 | bytes 18415476 | solution.py:122
  192.6 4.6 conditional.9
  198.5 4.6 conditional.9
  204.5 4.6 conditional.9
  210.3 4.6 conditional.9
  220.6 10.5 all-gather.14.cloned.1.call-done
  233.8 88.0 %all-gather.16.cloned.1.call-done = bf16[1152,3072]{1,0:T(8,128)(2,1)} async-done(((bf16[576,3072]{1,0:T(8,128)(2,1)}), bf16[1152,3072]{1,0:T(8,128)(2,1)}) %all-gather.16.cloned.1.call-update) | async-done | bytes 7077904 | tf_op jit(solution)/shard_map/all_gather | solution.py:286
  321.8 5.4 fusion.85
  327.2 85.3 %all-gather.18.cloned.1.call-done = bf16[1152,3072]{1,0:T(8,128)(2,1)} async-done(((bf16[576,3072]{1,0:T(8,128)(2,1)}), bf16[1152,3072]{1,0:T(8,128)(2,1)}) %all-gather.18.cloned.1.call-update) | async-done | bytes 7077904 | tf_op jit(solution)/shard_map/all_gather | solution.py:287
  412.5 5.5 fusion.86
  417.9 85.3 %all-gather.20.cloned.1.call-done = bf16[3072,1152]{1,0:T(8,128)(2,1)} async-done(((bf16[1536,1152]{1,0:T(8,128)(2,1)}), bf16[3072,1152]{1,0:T(8,128)(2,1)}) %all-gather.20.cloned.1.call-update) | async-done | bytes 7077904 | tf_op jit(solution)/shard_map/all_gather | solution.py:288
  503.3 6.9 multiply_convert_fusion
  510.2 6.0 fusion.87
  522.8 80.6 %while.60 = (s32[]{:T(128)}, f32[8,512,768]{2,1,0:T(8,128)}, s32[8]{0:T(128)S(1)}, s32[]{:T(128)}, s32[]{:T(128)}, /*index=5*/s32[128]{0:T(128)S(1)}, bf16[4096,...) while((s32[]{:T(128)}, f32[8,512,768]{2,1,0:T(8,128)}, ...), condition=%wide.region_20.21_spmd.clone, body=%wide.region_17.20_spmd.clone.sunk | while | flops 616563328 | bytes 47810428 | solution.py:253
  525.5 11.3 conditional.11
  532.3 4.3 fusion.50
  541.1 11.3 conditional.11
  556.6 11.3 conditional.11
  563.4 4.3 fusion.50
  572.2 11.3 conditional.11
  604.6 4.9 convolution_convert_fusion.2
  610.6 4.9 convolution_convert_fusion.1
  616.8 4.9 convolution_convert_fusion
  621.8 45.7 %while.59 = (s32[]{:T(128)}, f32[6,3,128,64]{2,3,1,0:T(8,128)S(1)}, s32[]{:T(128)}, s32[]{:T(128)}, s32[128]{0:T(128)S(1)}, /*index=5*/bf16[4096,384]{0,1:T(8,12...) while((s32[]{:T(128)}, f32[6,3,128,64]{2,3,1,0:T(8,128)S(1)}, ...), condition=%wide.region_16.17_spmd.clone, body=%wide.region_13.16_spmd.clone.sunk | while | flops 460554880 | bytes 14115669 | solution.py:190
  623.4 8.6 conditional.10
  633.3 8.6 conditional.10
  643.3 8.6 conditional.10
  653.2 8.9 conditional.10
  657.6 4.5 fusion.29
  672.7 129.0 %reduce-scatter.22.cloned.1.call-done = f32[128,768]{1,0:T(8,128)} async-done(((f32[4096,768]{1,0:T(8,128)}), f32[128,768]{1,0:T(8,128)}) %reduce-scatter.22.cloned.1.call-update) | async-done | bytes 393232 | tf_op jit(solution)/shard_map/reduce_scatter | solution.py:394
  806.7 83.4 %reduce-scatter.32.cloned.1.call-done = bf16[576,3072]{1,0:T(8,128)(2,1)} async-done(((bf16[1152,3072]{1,0:T(8,128)(2,1)}), bf16[576,3072]{1,0:T(8,128)(2,1)}) %reduce-scatter.32.cloned.1.call-update) | async-done | bytes 3538960 | tf_op jit(solution)/shard_map/reduce_scatter | solution.py:465
  890.2 6.3 copy.123
  896.6 81.4 %reduce-scatter.34.cloned.1.call-done = bf16[576,3072]{1,0:T(8,128)(2,1)} async-done(((bf16[1152,3072]{1,0:T(8,128)(2,1)}), bf16[576,3072]{1,0:T(8,128)(2,1)}) %reduce-scatter.34.cloned.1.call-update) | async-done | bytes 3538960 | tf_op jit(solution)/shard_map/reduce_scatter | solution.py:468
  977.9 6.3 copy.125
  984.4 81.6 %reduce-scatter.36.cloned.1.call-done = bf16[1536,1152]{1,0:T(8,128)(2,1)} async-done(((bf16[3072,1152]{1,0:T(8,128)(2,1)}), bf16[1536,1152]{1,0:T(8,128)(2,1)}) %reduce-scatter.36.cloned.1.call-update) | async-done | bytes 3538960 | tf_op jit(solution)/shard_map/reduce_scatter | solution.py:471
  1066.0 6.0 copy.127
  1078.7 5.0 fusion.57
  1083.7 22.4 %reduce-scatter.24.cloned.1.call-done = bf16[576,1152]{1,0:T(8,128)(2,1)} async-done(((bf16[1152,1152]{1,0:T(8,128)(2,1)}), bf16[576,1152]{1,0:T(8,128)(2,1)}) %reduce-scatter.24.cloned.1.call-update) | async-done | bytes 1327120 | tf_op jit(solution)/shard_map/reduce_scatter | solution.py:453
  1106.1 40.2 %reduce-scatter.30.cloned.1.call-done = bf16[576,1152]{1,0:T(8,128)(2,1)} async-done(((bf16[1152,1152]{1,0:T(8,128)(2,1)}), bf16[576,1152]{1,0:T(8,128)(2,1)}) %reduce-scatter.30.cloned.1.call-update) | async-done | bytes 1327120 | tf_op jit(solution)/shard_map/reduce_scatter | solution.py:462
  1149.7 40.4 %all-reduce.6 = (f32[1152]{0:T(1024)}, f32[1152]{0:T(1024)}) all-reduce(f32[1152]{0:T(1024)S(1)} %get-tuple-element.1592, f32[1152]{0:T(1024)S(1)} %get-tuple-element.1590), channel_id=1, replica_groups=mesh['ctx'=16,'fsdp'=2] {'ctx','fsdp'}, use_global_device_ids=true, to_apply=%region_38.39 | all-reduce | flops 2304 | bytes 18432 | tf_op jit(solution)/shard_map/psum | solution.py:484
  1191.2 180.7 %all-reduce.10 = (f32[576,1152]{1,0:T(8,128)}, f32[576,384]{1,0:T(8,128)S(1)}, f32[576,384]{1,0:T(8,128)S(1)}, f32[576,1152]{1,0:T(8,128)}) all-reduce(bf16[576,1152]{1,0:T(8,128)(2,1)} %reduce-scatter.24.cloned.1.call-done, ...), channel_id=4, replica_groups=mesh['ctx'=16,'fsdp'=2] {'ctx'}, use_global_device_ids=true, to_apply=%region_24.25.clone | all-reduce | flops 1769472 | bytes 10616832
  1376.8 58.7 %reduce-scatter.40.cloned.1.call-done = f32[192,576]{1,0:T(8,128)} async-done(((f32[3072,576]{1,0:T(8,128)}), f32[192,576]{1,0:T(8,128)}) %reduce-scatter.40.cloned.1.call-update) | async-done | bytes 442384
  1435.5 94.1 %reduce-scatter.42.cloned.1.call-done = f32[72,1536]{1,0:T(8,128)} async-done(((f32[1152,1536]{1,0:T(8,128)}), f32[72,1536]{1,0:T(8,128)}) %reduce-scatter.42.cloned.1.call-update) | async-done | bytes 442384
  (317 shorter events, 163.3 us)
Async XLA Ops:
  7.2 55.6 %copy-start.2 = (bf16[128,1152]{1,0:T(8,128)(2,1)S(1)}, bf16[128,1152]{1,0:T(8,128)(2,1)}, u32[]{:S(2)}) copy-start(bf16[128,1152]{1,0:T(8,128)(2,1)} %param.24) | copy-start | bytes 884740
  7.2 33.6 %copy-start.24 = (bf16[576,384]{1,0:T(8,128)(2,1)S(1)}, bf16[576,384]{1,0:T(8,128)(2,1)}, u32[]{:S(2)}) copy-start(bf16[576,384]{1,0:T(8,128)(2,1)} %param.26) | copy-start | bytes 1327108
  7.2 60.5 %all-gather.10.cloned.1.call-start = ((), (), s32[]{:S(2)}) async-start(), calls=%async_computation.12 | async-start | bytes 3981312 | tf_op jit(solution)/shard_map/all_gather | solution.py:282
  7.9 121.8 %all-gather.12.cloned.1.call-start = ((), (), s32[]{:S(2)}) async-start(), calls=%async_computation.13 | async-start | bytes 3244032 | tf_op jit(solution)/shard_map/all_gather | solution.py:340
  37.0 0.9 copy-start.13
  40.0 151.2 %all-gather.8.cloned.1.call-start = ((), (), s32[]{:S(2)}) async-start(), calls=%async_computation.11 | async-start | bytes 3244032 | tf_op jit(solution)/shard_map/all_gather | solution.py:339
  61.9 0.9 copy-start.12
  64.0 167.1 %all-gather.14.cloned.1.call-start = ((), (), s32[]{:S(2)}) async-start(), calls=%async_computation.14 | async-start | bytes 3981312 | tf_op jit(solution)/shard_map/all_gather | solution.py:285
  64.6 257.2 %all-gather.16.cloned.1.call-start = ((), (), s32[]{:S(2)}) async-start(), calls=%async_computation.15 | async-start | bytes 10616832 | tf_op jit(solution)/shard_map/all_gather | solution.py:286
  65.2 347.2 %all-gather.18.cloned.1.call-start = ((), (), s32[]{:S(2)}) async-start(), calls=%async_computation.16 | async-start | bytes 10616832 | tf_op jit(solution)/shard_map/all_gather | solution.py:287
  65.8 437.5 %all-gather.20.cloned.1.call-start = ((), (), s32[]{:S(2)}) async-start(), calls=%async_computation.17 | async-start | bytes 10616832 | tf_op jit(solution)/shard_map/all_gather | solution.py:288
  66.5 735.2 %reduce-scatter.22.cloned.1.call-start = ((), (), s32[]{:S(2)}) async-start(), calls=%async_computation.18 | async-start | bytes 12976128 | tf_op jit(solution)/shard_map/reduce_scatter | solution.py:394
  220.6 106.6 %copy-start.18 = (bf16[6,3,128,64]{2,3,1,0:T(8,128)(2,1)}, bf16[6,3,128,64]{2,3,1,0:T(8,128)(2,1)S(1)}, u32[]{:S(2)}) copy-start(bf16[6,3,128,64]{2,3,1,0:T(8,128)(2,1)S(1)} %fusion.71) | copy-start | bytes 884740
  233.6 285.2 %copy-start.6 = (f32[128,1152]{1,0:T(8,128)}, f32[128,1152]{1,0:T(8,128)S(1)}, u32[]{:S(2)}) copy-start(f32[128,1152]{1,0:T(8,128)S(1)} %get-tuple-element.1702) | copy-start | bytes 1769476
  233.8 178.7 %copy-start.4 = (bf16[128,1152]{1,0:T(8,128)(2,1)}, bf16[128,1152]{1,0:T(8,128)(2,1)S(1)}, u32[]{:S(2)}) copy-start(bf16[128,1152]{1,0:T(8,128)(2,1)S(1)} %multiply_convert_fusion.3) | copy-start | bytes 884740
  412.5 90.8 %copy-start.21 = (f32[128,3072]{1,0:T(8,128)S(1)}, f32[128,3072]{1,0:T(8,128)}, u32[]{:S(2)}) copy-start(f32[128,3072]{1,0:T(8,128)} %fusion.85) | copy-start | bytes 4718596
  510.2 6.0 copy-start.16
  510.2 8.6 copy-start.14
  510.2 6.0 copy-start.1
  516.2 2.6 copy-start.22
  516.2 3.7 copy-start.8
  519.0 0.8 copy-start.10
  527.9 2.2 copy-start
  543.5 2.2 copy-start
  559.0 2.2 copy-start
  574.6 2.2 copy-start
  603.3 1.0 copy-start.5
  603.3 1.2 copy-start.17
  603.4 286.8 %reduce-scatter.32.cloned.1.call-start = ((), (), s32[]{:S(2)}) async-start(), calls=%async_computation.23 | async-start | bytes 10616832 | tf_op jit(solution)/shard_map/reduce_scatter | solution.py:465
  609.5 1.1 copy-start.15
  609.5 368.4 %reduce-scatter.34.cloned.1.call-start = ((), (), s32[]{:S(2)}) async-start(), calls=%async_computation.24 | async-start | bytes 10616832 | tf_op jit(solution)/shard_map/reduce_scatter | solution.py:468
  615.6 1.1 copy-start.9
  615.6 1.2 copy-start.23
  615.6 450.4 %reduce-scatter.36.cloned.1.call-start = ((), (), s32[]{:S(2)}) async-start(), calls=%async_computation.25 | async-start | bytes 10616832 | tf_op jit(solution)/shard_map/reduce_scatter | solution.py:471
  621.7 484.4 %reduce-scatter.24.cloned.1.call-start = ((), (), s32[]{:S(2)}) async-start(), calls=%async_computation.19 | async-start | bytes 3981312 | tf_op jit(solution)/shard_map/reduce_scatter | solution.py:453
  621.8 45.8 %copy-start.3 = (bf16[128,1152]{1,0:T(8,128)(2,1)S(1)}, bf16[128,1152]{1,0:T(8,128)(2,1)}, u32[]{:S(2)}) copy-start(bf16[128,1152]{1,0:T(8,128)(2,1)} %param.24) | copy-start | bytes 884740
  667.5 2.6 copy-start.11
  667.5 2.6 copy-start.19
  670.1 476.3 %reduce-scatter.30.cloned.1.call-start = ((), (), s32[]{:S(2)}) async-start(), calls=%async_computation.22 | async-start | bytes 3981312 | tf_op jit(solution)/shard_map/reduce_scatter | solution.py:462
  672.6 518.6 %reduce-scatter.26.cloned.1.call-start = ((), (), s32[]{:S(2)}) async-start(), calls=%async_computation.20 | async-start | bytes 1327104 | tf_op jit(solution)/shard_map/reduce_scatter | solution.py:456
  804.3 386.9 %reduce-scatter.28.cloned.1.call-start = ((), (), s32[]{:S(2)}) async-start(), calls=%async_computation.21 | async-start | bytes 1327104 | tf_op jit(solution)/shard_map/reduce_scatter | solution.py:459
  806.7 570.1 %reduce-scatter.38.cloned.1.call-start = ((), (), s32[]{:S(2)}) async-start(), calls=%async_computation.26 | async-start | bytes 8355840
  896.5 539.0 %reduce-scatter.40.cloned.1.call-start = ((), (), s32[]{:S(2)}) async-start(), calls=%async_computation.27 | async-start | bytes 8355840
  984.3 545.3 %reduce-scatter.42.cloned.1.call-start = ((), (), s32[]{:S(2)}) async-start(), calls=%async_computation.28 | async-start | bytes 7520256
  1072.0 0.7 copy-start.25
  1072.0 6.7 copy-start.7
  1078.7 67.6 %copy-start.20 = (f32[128,1152]{1,0:T(8,128)S(1)}, f32[128,1152]{1,0:T(8,128)}, u32[]{:S(2)}) copy-start(f32[128,1152]{1,0:T(8,128)} %fusion.88) | copy-start | bytes 1769476
Sparse Core Ops, SparseCore 0:
  9.6 58.0 all-gather.9
  71.2 58.5 all-gather.11
  133.2 57.9 all-gather.7
  192.6 38.4 all-gather.13
  232.5 89.2 all-gather.15
  323.2 89.2 all-gather.17
  414.0 89.2 all-gather.19
  603.5 198.1 reduce-scatter.21
  804.1 86.0 reduce-scatter.31
  892.3 85.5 reduce-scatter.33
  980.4 85.5 reduce-scatter.35
  1068.1 37.9 reduce-scatter.23
  1108.4 37.9 reduce-scatter.29
  1148.5 19.0 reduce-scatter.25
  1169.7 18.5 reduce-scatter.27
  1192.7 131.2 reduce-scatter.37
  1328.5 106.9 reduce-scatter.39
  1439.9 89.6 reduce-scatter.41
where the time goes:
time: 1550 us; the launch traced here: 1540 us
  waiting for transfers between devices  979 us (63%)
  blocking collectives  266 us (17%)
  matrix products  138 us (9%)
  local copies, waits for them, and re-layouts  83.1 us (5%)
  loops' own time  38.8 us (3%)
  between operations  17.1 us (1%)
    unnamed x2, blocking collectives  185 us
    unnamed x21, waiting for transfers between devices  156 us
    reduce_scatter x1, waiting for transfers between devices, per_device(): lax.psum_scatter(key_grads(query_rows, grads_out, log_total, row_delta, l...  129 us
    all_gather x1, waiting for transfers between devices, per_device(): lax.all_gather(gate_weight, 'fsdp', axis=0, tiled=True)  88 us
    all_gather x1, waiting for transfers between devices, per_device(): lax.all_gather(down_weight, 'fsdp', axis=0, tiled=True)  85.3 us
    all_gather x1, waiting for transfers between devices, per_device(): lax.all_gather(up_weight, 'fsdp', axis=0, tiled=True)  85.3 us
    reduce_scatter x1, waiting for transfers between devices, per_device(): lax.psum_scatter(gate_partial.astype(jnp.bfloat16), 'fsdp', scatter_dimen...  83.4 us
    reduce_scatter x1, waiting for transfers between devices, per_device(): lax.psum_scatter(down_partial.astype(jnp.bfloat16), 'fsdp', scatter_dimen...  81.6 us
  transfers between devices with their start and end apart: 18, of which 15 were waited for; matrix products, arithmetic and copies ran while one was open for 9% of the time, Pallas kernels for 0%

commit v1 on v0

v1 whole, which is shorter than its diff:
```python
import functools
import math

import jax
import jax.numpy as jnp
from jax import lax
from jax.experimental import pallas as pl
from jax.experimental.pallas import tpu as pltpu
from jax.sharding import PartitionSpec as P

QUERY_HEADS = 18
KEY_VALUE_HEADS = 6
HEAD_SIZE = 64
HS = HEAD_SIZE

EPS = 1e-05
THETA = 10000.0
NEG = -1e30
AXES = ("ctx", "fsdp")


def rope_tables(positions):
    half_dim = HEAD_SIZE // 2
    frequency = jnp.exp(-math.log(THETA) * jnp.arange(half_dim, dtype=jnp.float32) / half_dim)
    angles = positions.astype(jnp.float32)[:, None] * frequency[None, :]
    return (jnp.cos(angles), jnp.sin(angles))


def apply_rotary(values, cosine_table, sine_table):
    half_dim = values.shape[-1] // 2
    first_half = values[..., :half_dim]
    second_half = values[..., half_dim:]
    cos_rows = cosine_table[:, None, :]
    sin_rows = sine_table[:, None, :]
    return jnp.concatenate(
        [
            first_half * cos_rows - second_half * sin_rows,
            second_half * cos_rows + first_half * sin_rows,
        ],
        axis=-1,
    )


def unrotate(values, cosine_table, sine_table):
    half_dim = values.shape[-1] // 2
    first_half = values[..., :half_dim]
    second_half = values[..., half_dim:]
    cos_rows = cosine_table[:, None, :]
    sin_rows = sine_table[:, None, :]
    return jnp.concatenate(
        [
            first_half * cos_rows + second_half * sin_rows,
            second_half * cos_rows - first_half * sin_rows,
        ],
        axis=-1,
    )


def doc_begin(indices, doc_starts):
    marked = jnp.where(indices[:, None] >= doc_starts[None, :], doc_starts[None, :], 0)
    return jnp.max(marked, axis=1)


def layout_rows(device, row_count):
    return device * row_count + jnp.arange(row_count, dtype=jnp.int32)


def heads_rows(natural):
    return jnp.transpose(natural.astype(jnp.float32))
def padded(rows, heads, g):
    top = jnp.concatenate([rows[HS*(heads*g+j):HS*(heads*g+j+1)] for j in range(heads)], axis=1)
    z = jnp.zeros_like(top)
    return jnp.concatenate([top, z] if g == 0 else [z, top], axis=0)
def head_lanes(per_group, heads, tq):
    return jnp.transpose(jnp.concatenate([per_group[g][:, tq*j:tq*(j+1)] for g in range(2) for j in range(heads)], axis=0))
def bias_tile(info, docs, first, bk, tq):
    query = info[0] + lax.broadcasted_iota(jnp.int32, (1, tq), 1)
    begin = jnp.zeros((1, tq), jnp.int32)
    for i in range(docs.shape[0]):
        begin = jnp.maximum(begin, jnp.where(query >= docs[i], docs[i], 0))
    key = first + lax.broadcasted_iota(jnp.int32, (bk, 1), 0)
    return jnp.where((key <= query) & (key >= begin), 0.0, NEG)

def fwd_kernel(info, docs, q_ref, k_ref, v_ref, o_ref, ot_ref, lse_ref, *, bk, heads, tq):
    rows = heads*tq
    qt = heads_rows(q_ref[...]) * (1.0/8.0)
    qg = [padded(qt, heads, g).astype(jnp.bfloat16) for g in range(2)]
    def body(j, carry):
        first = pl.multiple_of(j*bk, bk)
        kb = k_ref[pl.ds(first, bk), :]
        vt = jnp.transpose(v_ref[pl.ds(first, bk), :])
        bias = bias_tile(info, docs, first, bk, tq)
        bias = jnp.concatenate([bias]*heads, axis=1)
        out = []
        for g in range(2):
            m, l, acc = carry[g]
            s = jnp.dot(kb, qg[g], preferred_element_type=jnp.float32) + bias
            mn = jnp.maximum(m, jnp.max(s, axis=0, keepdims=True))
            p = jnp.exp(s - mn)
            a = jnp.exp(m - mn)
            l = l*a + jnp.sum(p, axis=0, keepdims=True)
            acc = acc*a + jnp.dot(vt[HS*g:HS*(g+1)], p.astype(jnp.bfloat16), preferred_element_type=jnp.float32)
            out.append((mn, l, acc))
        return tuple(out)
    init = tuple((jnp.full((1, rows), NEG, jnp.float32), jnp.zeros((1, rows), jnp.float32), jnp.zeros((HS, rows), jnp.float32)) for _ in range(2))
    res = lax.fori_loop(info[1], info[2], body, init)
    ots = []
    for g in range(2):
        m, l, acc = res[g]
        o = acc / l
        ots.append(o)
        ot_ref[g] = o
        lse_ref[g] = m + jnp.log(l)
    o_ref[...] = head_lanes(ots, heads, tq).astype(o_ref.dtype)

def bwd_kernel(info, docs, q_ref, do_ref, ot_ref, lse_ref, k_ref, v_ref, dq_ref, dk_ref, dv_ref, acc_ref, *, bk, heads, tq):
    rows = heads*tq
    n = k_ref.shape[0]
    qt = heads_rows(q_ref[...]) * (1.0/8.0)
    dt = heads_rows(do_ref[...])
    qg = [padded(qt, heads, g) for g in range(2)]
    dg = [padded(dt, heads, g) for g in range(2)]
    qrows = jnp.concatenate([jnp.transpose(x) for x in qg], axis=0).astype(jnp.bfloat16)
    drows = jnp.concatenate([jnp.transpose(x) for x in dg], axis=0).astype(jnp.bfloat16)
    delta = [jnp.sum(dg[g][HS*g:HS*(g+1)] * ot_ref[g], axis=0, keepdims=True) for g in range(2)]
    lse = [lse_ref[g] for g in range(2)]
    qg = [x.astype(jnp.bfloat16) for x in qg]
    dg = [x.astype(jnp.bfloat16) for x in dg]
    acc_ref[...] = jnp.zeros_like(acc_ref)
    def zero(j, _):
        first = pl.multiple_of(j*bk, bk)
        dk_ref[pl.ds(first, bk), :] = jnp.zeros((bk, 2*HS), dk_ref.dtype)
        dv_ref[pl.ds(first, bk), :] = jnp.zeros((bk, 2*HS), dv_ref.dtype)
        return _
    lax.fori_loop(0, info[1], zero, 0)
    lax.fori_loop(info[2], n//bk, zero, 0)
    def body(j, _):
        first = pl.multiple_of(j*bk, bk)
        kb = k_ref[pl.ds(first, bk), :]
        vb = v_ref[pl.ds(first, bk), :]
        kt = jnp.transpose(kb)
        bias = bias_tile(info, docs, first, bk, tq)
        bias = jnp.concatenate([bias]*heads, axis=1)
        ps = []; dss = []
        for g in range(2):
            s = jnp.dot(kb, qg[g], preferred_element_type=jnp.float32)
            p = jnp.exp(s + (bias - lse[g]))
            dp = jnp.dot(vb, dg[g], preferred_element_type=jnp.float32)
            ds = (p * (dp - delta[g])).astype(jnp.bfloat16)
            ps.append(p.astype(jnp.bfloat16)); dss.append(ds)
            acc_ref[g] += jnp.dot(kt[HS*g:HS*(g+1)], ds, preferred_element_type=jnp.float32)
        dv = jnp.dot(jnp.concatenate(ps, axis=1), drows, preferred_element_type=jnp.float32)
        dk = jnp.dot(jnp.concatenate(dss, axis=1), qrows, preferred_element_type=jnp.float32)
        dk_ref[pl.ds(first, bk), :] = dk.astype(dk_ref.dtype)
        dv_ref[pl.ds(first, bk), :] = dv.astype(dv_ref.dtype)
        return _
    lax.fori_loop(info[1], info[2], body, 0)
    dq_ref[...] = head_lanes([acc_ref[g] for g in range(2)], heads, tq) * (1.0/8.0)

def attention_forward(info, docs, q, kv, bk=512):
    tq, width = q.shape
    n = kv.shape[0]
    parts = kv.shape[1]//(4*HS)
    heads = width//HS//(2*parts)
    smem = pl.BlockSpec(memory_space=pltpu.SMEM)
    return pl.pallas_call(
        functools.partial(fwd_kernel, bk=bk, heads=heads, tq=tq),
        grid=(parts,),
        out_shape=[jax.ShapeDtypeStruct((tq, width), jnp.bfloat16), jax.ShapeDtypeStruct((2*parts, HS, heads*tq), jnp.float32), jax.ShapeDtypeStruct((2*parts, 1, heads*tq), jnp.float32)],
        in_specs=[smem, smem, pl.BlockSpec((tq, 2*heads*HS), lambda p: (0, p)), pl.BlockSpec((n, 2*HS), lambda p: (0, p)), pl.BlockSpec((n, 2*HS), lambda p: (0, parts + p))],
        out_specs=[pl.BlockSpec((tq, 2*heads*HS), lambda p: (0, p)), pl.BlockSpec((2, HS, heads*tq), lambda p: (p, 0, 0)), pl.BlockSpec((2, 1, heads*tq), lambda p: (p, 0, 0))],
        compiler_params=pltpu.CompilerParams(vmem_limit_bytes=60*2**20),
        name="attention_forward",
    )(info, docs, q, kv, kv)

def attention_backward(info, docs, q, do, ot, lse, kv, bk=512):
    tq, width = q.shape
    n = kv.shape[0]
    parts = kv.shape[1]//(4*HS)
    heads = width//HS//(2*parts)
    buffers = 2 if 32 * n * HS <= 40*2**20 else 1
    smem = pl.BlockSpec(memory_space=pltpu.SMEM)
    return pl.pallas_call(
        functools.partial(bwd_kernel, bk=bk, heads=heads, tq=tq),
        grid=(parts,),
        out_shape=[jax.ShapeDtypeStruct((tq, width), jnp.float32), jax.ShapeDtypeStruct((n, 2*parts*HS), jnp.bfloat16), jax.ShapeDtypeStruct((n, 2*parts*HS), jnp.bfloat16)],
        in_specs=[smem, smem, pl.BlockSpec((tq, 2*heads*HS), lambda p: (0, p)), pl.BlockSpec((tq, 2*heads*HS), lambda p: (0, p)),
                  pl.BlockSpec((2, HS, heads*tq), lambda p: (p, 0, 0)), pl.BlockSpec((2, 1, heads*tq), lambda p: (p, 0, 0)),
                  pl.BlockSpec((n, 2*HS), lambda p: (0, p), pipeline_mode=pl.Buffered(buffers)), pl.BlockSpec((n, 2*HS), lambda p: (0, parts + p), pipeline_mode=pl.Buffered(buffers))],
        out_specs=[pl.BlockSpec((tq, 2*heads*HS), lambda p: (0, p)), pl.BlockSpec((n, 2*HS), lambda p: (0, p)), pl.BlockSpec((n, 2*HS), lambda p: (0, p))],
        scratch_shapes=[pltpu.VMEM((2, HS, heads*tq), jnp.float32)],
        compiler_params=pltpu.CompilerParams(vmem_limit_bytes=60*2**20),
        name="attention_backward",
    )(info, docs, q, do, ot, lse, kv, kv)


def exchange_kernel(nctx, nf, blocks, small, out, small_out, own_sem, send_sem, recv_sem):
    me_c, me_f = lax.axis_index("ctx"), lax.axis_index("fsdp")
    me = me_c * nf + me_f
    n = nctx * nf
    barrier = pltpu.get_barrier_semaphore()

    def target(k):
        other = lax.rem(me + k, n)
        return other, {"ctx": other // nf, "fsdp": lax.rem(other, nf)}

    def greet(k, carry):
        _, where = target(k)
        pl.semaphore_signal(barrier, inc=1, device_id=where, device_id_type=pl.DeviceIdType.MESH)
        return carry

    lax.fori_loop(1, n, greet, 0)
    own = pltpu.make_async_copy(blocks.at[me_c], out.at[me], own_sem.at[0])
    own.start()
    own_small = pltpu.make_async_copy(small, small_out.at[me], own_sem.at[1])
    own_small.start()
    pl.semaphore_wait(barrier, n - 1)

    def copies(k):
        other, where = target(k)
        return (
            pltpu.make_async_remote_copy(
                src_ref=blocks.at[other // nf], dst_ref=out.at[me],
                send_sem=send_sem.at[0, k], recv_sem=recv_sem.at[0, k],
                device_id=where, device_id_type=pl.DeviceIdType.MESH,
            ),
            pltpu.make_async_remote_copy(
                src_ref=small, dst_ref=small_out.at[me],
                send_sem=send_sem.at[1, k], recv_sem=recv_sem.at[1, k],
                device_id=where, device_id_type=pl.DeviceIdType.MESH,
            ),
        )

    def begin(k, carry):
        for copy in copies(k):
            copy.start()
        return carry

    def finish(k, carry):
        for copy in copies(k):
            copy.wait()
        return carry

    lax.fori_loop(1, n, begin, 0)
    lax.fori_loop(1, n, finish, 0)
    own.wait()
    own_small.wait()


def exchange(blocks, small, nctx, nf):
    n = nctx * nf
    vmem = pl.BlockSpec(memory_space=pltpu.VMEM)
    return pl.pallas_call(
        functools.partial(exchange_kernel, nctx, nf),
        out_shape=[
            jax.ShapeDtypeStruct((n,) + blocks.shape[1:], blocks.dtype),
            jax.ShapeDtypeStruct((n,) + small.shape, small.dtype),
        ],
        in_specs=[vmem, vmem],
        out_specs=[vmem, vmem],
        scratch_shapes=[
            pltpu.SemaphoreType.DMA((2,)),
            pltpu.SemaphoreType.DMA((2, n)),
            pltpu.SemaphoreType.DMA((2, n)),
        ],
        compiler_params=pltpu.CompilerParams(
            collective_id=0, has_side_effects=True, vmem_limit_bytes=48 * 2**20
        ),
        name="exchange",
    )(blocks, small)


def line_dims(count):
    fours = 0
    while count % 4 == 0:
        count //= 4
        fours += 1
    return ([count] if count > 1 else []) + [4] * fours


class Layout:
    def __init__(self, nctx, nf):
        self.nctx, self.nf, self.plane = nctx, nf, nctx // 2
        self.ctx = lax.axis_index("ctx")
        self.f = lax.axis_index("fsdp")
        self.core = lax.rem(self.ctx, 2)
        self.place = self.ctx // 2

    def send(self, value, move):
        pairs = []
        for ctx in range(self.nctx):
            for f in range(self.nf):
                place, core, side = move(ctx // 2, ctx % 2, f)
                pairs.append((ctx * self.nf + f, (place * 2 + core) * self.nf + side))
        return lax.ppermute(value, AXES, pairs)

    def to_core(self, value):
        return self.send(value, lambda r, c, f: (r, 1 - c, f))

    def to_side(self, value):
        return self.send(value, lambda r, c, f: (r, c, 1 - f))

    def in_order(self, which, own, other, axis=0):
        return jnp.where(
            which == 0,
            jnp.concatenate([own, other], axis=axis),
            jnp.concatenate([other, own], axis=axis),
        )

    def plane_scatter(self, data):
        stride = 1
        for size in line_dims(self.plane):
            coord = lax.rem(self.place // stride, size)
            data = data.reshape((data.shape[0] // size, size) + data.shape[1:])
            total = lax.dynamic_index_in_dim(data, coord, 1, keepdims=False).astype(jnp.float32)
            for k in range(1, size):
                part = lax.dynamic_index_in_dim(data, lax.rem(coord + k, size), 1, keepdims=False)

                def move(r, c, f, k=k, size=size, stride=stride):
                    at = r // stride % size
                    return r + ((at + k) % size - at) * stride, c, f

                total = total + self.send(part, move).astype(jnp.float32)
            stride *= size
            data = total if data.shape[0] == 1 else total.astype(jnp.bfloat16)
        return data[0]


def pair_weight(lay, local):
    half = local.shape[0] // 2
    mine = lax.dynamic_slice_in_dim(local, lay.core * half, half, 0)
    got = lay.to_side(mine)
    other = lay.to_core(got)
    return lay.in_order(lay.f, local, lay.in_order(lay.core, got, other))


def gather_group(lay, own):
    two = jnp.concatenate([own, lay.to_side(own)], axis=0)
    return jnp.concatenate([two, lay.to_core(two)], axis=0)


def scatter_group(lay, partial, rows):
    got = lay.to_core(partial[2 * rows :].astype(jnp.bfloat16))
    total = partial[: 2 * rows] + got.astype(jnp.float32)
    last = lay.to_side(total[rows:].astype(jnp.bfloat16))
    return total[:rows] + last.astype(jnp.float32)


def column_blocks(values, count):
    rows, width = values.shape
    return values.reshape(rows, count, width // count)


def per_device(
    nctx,
    nf,
    tokens,
    query_weight,
    key_projection,
    value_projection,
    output_weight,
    gate_weight,
    up_weight,
    down_weight,
    norm_attn,
    norm_mlp,
    doc_starts,
    cotangent,
):
    lay = Layout(nctx, nf)
    f, core = lay.f, lay.core
    token_rows, width = tokens.shape
    half = width // nf
    n_tokens = token_rows * nctx * nf
    hidden_units = gate_weight.shape[1]
    quarter = hidden_units // (2 * nf)
    bf16, f32 = jnp.bfloat16, jnp.float32

    gains = jnp.stack([norm_attn, norm_mlp])
    gains = lay.in_order(f, gains, lay.to_side(gains), axis=1).astype(f32)
    gain_attn, gain_mlp = gains[0], gains[1]
    qkv_full = pair_weight(
        lay, jnp.concatenate([query_weight, key_projection, value_projection], axis=1)
    )
    output_full = pair_weight(lay, output_weight)

    def quarter_columns(index):
        at = index * quarter
        return jnp.concatenate(
            [
                lax.dynamic_slice_in_dim(gate_weight, at, quarter, 1),
                lax.dynamic_slice_in_dim(up_weight, at, quarter, 1),
            ],
            axis=1,
        )

    mine = 2 * f + core
    gate_up = lay.in_order(
        f, quarter_columns(mine), lay.to_side(quarter_columns(2 * (1 - f) + core))
    )
    down = lax.dynamic_slice_in_dim(down_weight, core * quarter, quarter, 0)
    cotangents = gather_group(lay, cotangent)

    hidden = tokens.astype(f32)
    inv_attn = lax.rsqrt(jnp.mean(hidden * hidden, axis=-1, keepdims=True) + EPS)
    normed_attn = hidden * inv_attn
    attention_input = (normed_attn * gain_attn).astype(bf16)

    def pair_side(values):
        halves = values.reshape(token_rows, nf, half)
        own = lax.dynamic_index_in_dim(halves, f, 1, keepdims=False)
        other = lax.dynamic_index_in_dim(halves, 1 - f, 1, keepdims=False)
        return lay.in_order(f, own, lay.to_side(other))

    own_device = lax.axis_index(AXES)
    own_index = layout_rows(own_device, token_rows)
    own_begin = doc_begin(own_index, doc_starts)
    cosine_table, sine_table = rope_tables(own_index - own_begin)

    qkv = jnp.dot(attention_input, qkv_full, preferred_element_type=f32)
    query_width = QUERY_HEADS * HEAD_SIZE
    key_width = KEY_VALUE_HEADS * HEAD_SIZE
    rotated = apply_rotary(
        qkv[:, : query_width + key_width].reshape(
            token_rows, QUERY_HEADS + KEY_VALUE_HEADS, HEAD_SIZE
        ),
        cosine_table,
        sine_table,
    ).astype(bf16).reshape(token_rows, query_width + key_width)
    query_rot = rotated[:, :query_width]
    key_value = jnp.concatenate(
        [rotated[:, query_width:], qkv[:, query_width + key_width :].astype(bf16)], axis=1
    )
    key_values = lax.all_gather(key_value, AXES, axis=0, tiled=True)
    block = math.gcd(n_tokens, 512)
    start = own_device * token_rows
    info = jnp.stack(
        [start, jnp.min(own_begin) // block, (start + token_rows - 1) // block + 1]
    ).astype(jnp.int32)
    attn_low, attn_exact, log_total = attention_forward(
        info, doc_starts, query_rot, key_values, block
    )

    resid = hidden + jnp.dot(attn_low, output_full, preferred_element_type=f32)
    inv_mlp = lax.rsqrt(jnp.mean(resid * resid, axis=-1, keepdims=True) + EPS)
    normed_mlp = resid * inv_mlp
    mlp_in = (normed_mlp * gain_mlp).astype(bf16)
    mlp_ins = gather_group(lay, mlp_in)
    gate_up_pre = jnp.dot(mlp_ins, gate_up, preferred_element_type=f32)
    gate_pre, up_pre = gate_up_pre[:, :quarter], gate_up_pre[:, quarter:]
    sigmoid_gate = jax.nn.sigmoid(gate_pre)
    gate_act = jax.nn.silu(gate_pre)
    mixed = (gate_act * up_pre).astype(bf16)
    grad_mixed = jnp.einsum("td,fd->tf", cotangents, down, preferred_element_type=f32)
    grad_gate = (grad_mixed * up_pre * sigmoid_gate * (1.0 + gate_pre * (1.0 - sigmoid_gate))).astype(bf16)
    grad_up = (grad_mixed * gate_act).astype(bf16)
    grads = jnp.concatenate([grad_gate, grad_up], axis=1)
    grad_mlp_in = scatter_group(
        lay, jnp.einsum("tf,df->td", grads, gate_up, preferred_element_type=f32), token_rows
    )
    result = (
        resid
        + scatter_group(lay, jnp.dot(mixed, down, preferred_element_type=f32), token_rows)
    ).astype(bf16)

    gain_mlp_partial = jnp.sum(grad_mlp_in * normed_mlp, axis=0)
    scaled_mlp = grad_mlp_in * gain_mlp
    grad_resid = cotangent.astype(f32) + inv_mlp * (
        scaled_mlp - normed_mlp * jnp.mean(scaled_mlp * normed_mlp, axis=-1, keepdims=True)
    )
    grad_branch = grad_resid.astype(bf16)
    grad_attn = jnp.einsum(
        "td,hd->th", grad_branch, output_full, preferred_element_type=f32
    ).astype(bf16)

    grad_query_rot, grad_key_rot, grad_value_all = attention_backward(
        info, doc_starts, query_rot, grad_attn, attn_exact, log_total, key_values, block
    )
    grad_kv = jnp.concatenate([grad_key_rot, grad_value_all], axis=1).reshape(
        lay.plane, 2, nf, token_rows, 2 * key_width
    )
    own = lax.dynamic_index_in_dim(grad_kv, core, 1, keepdims=False).astype(f32)
    own = own + lay.to_core(
        lax.dynamic_index_in_dim(grad_kv, 1 - core, 1, keepdims=False)
    ).astype(f32)
    own = own.astype(bf16)
    both = lax.dynamic_index_in_dim(own, f, 1, keepdims=False).astype(f32)
    both = both + lay.to_side(lax.dynamic_index_in_dim(own, 1 - f, 1, keepdims=False)).astype(f32)
    grad_kv = lay.plane_scatter(both.astype(bf16))

    gate_up_partial = jnp.einsum("tf,td->fd", grads, mlp_ins, preferred_element_type=f32).astype(bf16)
    down_partial = jnp.einsum("td,tf->df", cotangents, mixed, preferred_element_type=f32).astype(bf16)
    gate_up_piece = lay.plane_scatter(
        gate_up_partial.reshape(2, lay.plane, quarter // lay.plane, width).transpose(1, 0, 2, 3)
    ).astype(bf16)
    down_piece = lay.plane_scatter(
        down_partial.reshape(lay.plane, width // lay.plane, quarter)
    )
    parity = lax.rem(lay.place, 2)
    left, right = gate_up_piece[..., :half], gate_up_piece[..., half:]
    per_side = lay.plane // 2

    def home(flip):
        def move(r, c, side):
            at = (2 * side + c) * per_side + r // 2
            return at // 2, at % 2, (r + flip) % 2

        return move

    same = lay.send(jnp.where(parity == 0, left, right), home(0))
    cross = lay.send(jnp.where(parity == 0, right, left), home(1))
    gate_up_sum = lay.in_order(f, same, cross, axis=1).astype(f32)
    gate_sum, up_sum = gate_up_sum[0].T, gate_up_sum[1].T
    down_piece = down_piece.reshape(2, width // nctx, quarter)
    down_own = lax.dynamic_index_in_dim(down_piece, core, 0, keepdims=False)
    down_other = lay.to_core(
        lax.dynamic_index_in_dim(down_piece, 1 - core, 0, keepdims=False).astype(bf16)
    ).astype(f32)
    down_sum = lay.in_order(core, down_own, down_other, axis=1).T

    grad_query = unrotate(
        grad_query_rot.reshape(token_rows, QUERY_HEADS, HEAD_SIZE), cosine_table, sine_table
    ).astype(bf16).reshape(token_rows, query_width)
    grad_key = unrotate(
        grad_kv[:, :key_width].reshape(token_rows, KEY_VALUE_HEADS, HEAD_SIZE),
        cosine_table,
        sine_table,
    ).astype(bf16).reshape(token_rows, key_width)
    grad_value = grad_kv[:, key_width:].astype(bf16)
    grad_qkv = jnp.concatenate([grad_query, grad_key, grad_value], axis=1)
    grad_attn_in = jnp.einsum("th,dh->td", grad_qkv, qkv_full, preferred_element_type=f32)
    gain_attn_partial = jnp.sum(grad_attn_in * normed_attn, axis=0)
    scaled_attn = grad_attn_in * gain_attn
    tokens_grad = grad_resid + inv_attn * (
        scaled_attn - normed_attn * jnp.mean(scaled_attn * normed_attn, axis=-1, keepdims=True)
    )

    inputs_all = lax.all_gather(pair_side(attention_input), "ctx", axis=0, tiled=True)
    attn_all = lax.all_gather(pair_side(attn_low), "ctx", axis=0, tiled=True)
    blocks = jnp.concatenate(
        [column_blocks(v, nctx) for v in (grad_query, grad_key, grad_value, grad_branch)], axis=2
    )
    used = blocks.shape[2]
    blocks = jnp.pad(blocks, ((0, 0), (0, 0), (0, -used % 128))).transpose(1, 0, 2)
    small = jnp.stack([gain_attn_partial, gain_mlp_partial])
    small = jnp.pad(small, ((0, 6), (0, 0)))
    columns, gain_parts = exchange(blocks, small, nctx, nf)
    columns = columns.reshape(n_tokens, -1)
    gain_sums = jnp.sum(gain_parts, axis=0)
    sizes = [query_width // nctx, key_width // nctx, key_width // nctx]
    qkv_cols = sum(sizes)
    qkv_sum = jnp.einsum("td,th->dh", inputs_all, columns[:, :qkv_cols], preferred_element_type=f32)
    output_sum = jnp.einsum(
        "th,td->hd", attn_all, columns[:, qkv_cols:used], preferred_element_type=f32
    )
    query_sum = qkv_sum[:, : sizes[0]]
    key_sum = qkv_sum[:, sizes[0] : sizes[0] + sizes[1]]
    value_sum = qkv_sum[:, sizes[0] + sizes[1] :]
    return (
        result,
        tokens_grad,
        query_sum,
        key_sum,
        value_sum,
        output_sum,
        gate_sum,
        up_sum,
        down_sum,
        gain_sums[0],
        gain_sums[1],
    )


def solution(mesh):
    return jax.shard_map(
        functools.partial(per_device, mesh.shape["ctx"], mesh.shape["fsdp"]),
        mesh=mesh,
        in_specs=(
            P(("ctx", "fsdp"), None),
            P("fsdp", None),
            P("fsdp", None),
            P("fsdp", None),
            P("fsdp", None),
            P("fsdp", None),
            P("fsdp", None),
            P("fsdp", None),
            P("fsdp"),
            P("fsdp"),
            P(),
            P(("ctx", "fsdp"), None),
        ),
        out_specs=(
            P(("ctx", "fsdp"), None),
            P(("ctx", "fsdp"), None),
            P("fsdp", "ctx"),
            P("fsdp", "ctx"),
            P("fsdp", "ctx"),
            P("fsdp", "ctx"),
            P("fsdp", "ctx"),
            P("fsdp", "ctx"),
            P("fsdp", "ctx"),
            P(),
            P(),
        ),
        check_vma=False,
    )
```

time: 1550 us -> 568 us (0.37)
  waiting for transfers between devices: 979 us -> 176 us
  blocking collectives: 266 us -> 0 us
  Pallas kernels: 0 us -> 124 us
  matrix products: 138 us -> 46.9 us
  starting transfers between devices: 0.73 us -> 74.1 us
  other arithmetic: 13.1 us -> 53.7 us
  loops' own time: 38.8 us -> 0 us
  local copies, waits for them, and re-layouts: 83.1 us -> 67.6 us
    reduce_scatter x8 -> x0, waiting for transfers between devices: 438 us -> none  [the longest x1 129 us: per_device(): lax.psum_scatter(key_grads(query_rows, grads_out, log_total, row_delta, l...]
    all_gather x7 -> x3, waiting for transfers between devices: 385 us -> 43.5 us  [the longest x1 43.5 us: per_device(): key_values = lax.all_gather(key_value, AXES, axis=0, tiled=True)]
    unnamed x2 -> x0, blocking collectives: 185 us -> none
    unnamed x21 -> x3, waiting for transfers between devices: 156 us -> 0.05 us
    ppermute x0 -> x33, waiting for transfers between devices: none -> 132 us  [send(): return lax.ppermute(value, AXES, pairs)]
    pallas_call x0 -> x3, Pallas kernels: none -> 124 us  [the longest x1 88.4 us: exchange(): pl.pallas_call(functools.partial(exchange_kernel, nctx, nf), out_shape=[j...]
    dot_general x48 -> x11, matrix products: 137 us -> 45.2 us  [the longest x1 7.73 us: per_device(): jnp.einsum('th,dh->td', grad_qkv, qkv_full, preferred_element_type=f32)]
    ppermute x0 -> x33, starting transfers between devices: none -> 73.8 us  [send(): return lax.ppermute(value, AXES, pairs)]
  transfers between devices with their start and end apart: 18 -> 36, of which waited for: 15 -> 15; matrix products, arithmetic and copies ran while one was open for 9% -> 24% of each run, Pallas kernels for 0% -> 22%
where the time goes in v1:
time: 568 us; the launch traced here: 562 us
  waiting for transfers between devices  176 us (31%)
  Pallas kernels  124 us (22%)
  starting transfers between devices  74.1 us (13%)
  local copies, waits for them, and re-layouts  67.6 us (12%)
  other arithmetic  53.7 us (9%)
  matrix products  46.9 us (8%)
  between operations  19.4 us (3%)
    ppermute x33, waiting for transfers between devices, send(): return lax.ppermute(value, AXES, pairs)  132 us
    pallas_call x1, Pallas kernels, exchange(): pl.pallas_call(functools.partial(exchange_kernel, nctx, nf), out_shape=[j...  88.4 us
    ppermute x33, starting transfers between devices, send(): return lax.ppermute(value, AXES, pairs)  73.8 us
    all_gather x1, waiting for transfers between devices, per_device(): key_values = lax.all_gather(key_value, AXES, axis=0, tiled=True)  43.5 us
    pallas_call x1, Pallas kernels, attention_backward(): pl.pallas_call(functools.partial(bwd_kernel, bk=bk, heads=heads, tq=tq),...  21.3 us
    unnamed x122, local copies, waits for them, and re-layouts  21.1 us
    pallas_call x1, Pallas kernels, attention_forward(): pl.pallas_call(functools.partial(fwd_kernel, bk=bk, heads=heads, tq=tq),...  14.7 us
  transfers between devices with their start and end apart: 36, of which 15 were waited for; matrix products, arithmetic and copies ran while one was open for 24% of the time, Pallas kernels for 22%

profile of v1, /device:TPU:15, one launch (start us, length us, event | category | flops | bytes accessed | tf_op | source)
XLA Modules:
  0.0 561.7 jit_solution(1855468180170481273)
XLA Ops:
  8.1 2.7 constant_dynamic-update-slice_fusion.2
  14.6 2.3 constant_dynamic-slice_fusion.18
  21.1 21.4 %collective-permute-done.1 = bf16[288,1920]{1,0:T(8,128)(2,1)} collective-permute-done((bf16[288,1920]{1,0:T(8,128)(2,1)}, bf16[288,1920]{1,0:T(8,128)(2,1)}, u32[]{:S(2)}, u32[]{:S(2)}) %collective-permute-start.1) | collective-permute-done | bytes 1105952 | tf_op jit(solution)/shard_map/ppermute | solution.py:295
  48.4 2.9 maximum_select_fusion.3
  51.4 2.1 fusion.28
  55.2 2.3 copy.60
  63.5 2.0 constant_dynamic-slice_fusion.17
  65.7 18.0 %collective-permute-done.3 = bf16[288,1152]{1,0:T(8,128)(2,1)} collective-permute-done((bf16[288,1152]{1,0:T(8,128)(2,1)}, bf16[288,1152]{1,0:T(8,128)(2,1)}, u32[]{:S(2)}, u32[]{:S(2)}) %collective-permute-start.3) | collective-permute-done | bytes 663584 | tf_op jit(solution)/shard_map/ppermute | solution.py:295
  84.5 3.4 constant_dynamic-slice_fusion.15
  97.7 3.2 maximum_select_fusion.4
  103.5 43.5 %all-gather.4.cloned.1.call-done.k_ref.v_ref = bf16[4096,768]{1,0:T(8,128)(2,1)} async-done(((bf16[128,768]{1,0:T(8,128)(2,1)}), bf16[4096,768]{1,0:T(8,128)(2,1)}) %all-gather.4.cloned.1.call-update) | async-done | bytes 6291472 | tf_op jit(solution)/shard_map/all_gather | solution.py:434
  147.0 14.7 %attention_forward.1 = (bf16[128,1152]{1,0:T(8,128)(2,1)}, f32[6,64,384]{2,1,0:T(8,128)}, f32[6,1,384]{2,1,0:T(1,128)}) custom-call(s32[3]{0:T(128)} %pad_add_fusion.info, s32[4]{0:T(128)} %docs.3, bf16[128,1152]{1,0:T(8,128)(2,1)} %copy.79.q_ref, bf16[4096,768]{1,0:T(8,128)(2,1)} %all-gather.4.cloned.1.call-done.k_ref.v_ref, ...), custom_call_target="tpu_custom_call" | custom-call | tf_op jit(solution)/shard_map/attention_forward/pallas_call | solution.py:166
  161.8 3.8 multiply_reduce_fusion.2
  173.0 3.0 collective-permute-done.5
  182.3 1.9 constant_dynamic-update-slice_fusion.3
  184.3 7.4 %fusion.44 = f32[512,1536]{1,0:T(8,128)S(1)} fusion(bf16[256,1152]{1,0:T(8,128)(2,1)} %collective-permute-done.6, bf16[128,1152]{1,0:T(8,128)(2,1)} %collective-permute-done.5, bf16[128,1152]{1,0:T(8,128)(2,1)} %multiply_convert_fusion.3, bf16[576,1536]{1,0:T(8,128)(2,1)} %collective-permute-done.7, bf16[576,768]{1,0:T(8,128)(2,1)} %get-tuple-element.87, ...), kind=kOutput, calls=%fused_computation.94 | convolution fusion | flops 1838481408 | bytes 7864321 | tf_op jit(solution)/shard_map/dot_general | solution.py:449
  193.5 5.2 fusion.22
  207.6 5.9 %collective-permute-done.13 = bf16[128,1152]{1,0:T(8,128)(2,1)S(1)} collective-permute-done((bf16[128,1152]{1,0:T(8,128)(2,1)S(1)}, bf16[128,1152]{1,0:T(8,128)(2,1)S(1)}, u32[]{:S(2)}, u32[]{:S(2)}) %collective-permute-start.13) | collective-permute-done | bytes 294944 | tf_op jit(solution)/shard_map/ppermute | solution.py:295
  214.3 5.5 collective-permute-done.9
  219.8 2.2 fusion.58
  223.7 21.3 %attention_backward.1 = (f32[128,1152]{1,0:T(8,128)}, bf16[4096,384]{1,0:T(8,128)(2,1)}, bf16[4096,384]{1,0:T(8,128)(2,1)}) custom-call(s32[3]{0:T(128)} %pad_add_fusion.info, s32[4]{0:T(128)} %docs.3, bf16[128,1152]{1,0:T(8,128)(2,1)} %copy.79.q_ref, bf16[128,1152]{1,0:T(8,128)(2,1)} %convolution_convert_fusion.2.do_ref, ...), custom_call_target="tpu_custom_call" | custom-call | tf_op jit(solution)/shard_map/attention_backward/pallas_call | solution.py:183
  244.9 3.3 pad_maximum_fusion
  248.3 2.3 constant_dynamic-slice_fusion.12
  250.6 2.0 copy.87
  253.4 2.6 convolution_convert_fusion.1
  258.4 4.3 collective-permute-done.21
  263.6 3.7 convolution_convert_fusion
  270.1 2.1 copy.63
  272.3 6.4 %collective-permute-done.28 = bf16[4,144,768]{2,1,0:T(8,128)(2,1)} collective-permute-done((bf16[4,144,768]{2,1,0:T(8,128)(2,1)}, bf16[4,144,768]{2,1,0:T(8,128)(2,1)}, u32[]{:S(2)}, u32[]{:S(2)}) %collective-permute-start.28) | collective-permute-done | bytes 884768 | tf_op jit(solution)/shard_map/ppermute | solution.py:295
  281.2 31.1 %collective-permute-start.30 = (bf16[1,144,768]{2,1,0:T(8,128)(2,1)}, bf16[1,144,768]{2,1,0:T(8,128)(2,1)}, u32[]{:S(2)}, u32[]{:S(2)}) collective-permute-start(bf16[1,144,768]{2,1,0:T(8,128)(2,1)} %get-tuple-element.99), channel_id=1, source_target_pairs={{0,16},{1,17},{2,18},{3,19},{4,20},{5,21},{6,22},{7,23},{8,24},{9,... | collective-permute-start | bytes 663560 | tf_op jit(solution)/shard_map/ppermute | solution.py:295
  312.3 2.4 collective-permute-start.29
  314.7 2.9 fusion
  324.4 2.0 copy.73
  328.1 2.0 copy.70
  331.4 3.6 collective-permute-done.29
  338.6 2.0 fusion.1
  341.9 18.5 %collective-permute-start.24 = (bf16[1,2,96,1152]{3,2,1,0:T(8,128)(2,1)}, bf16[1,2,96,1152]{3,2,1,0:T(8,128)(2,1)}, u32[]{:S(2)}, u32[]{:S(2)}) collective-permute-start(bf16[1,2,96,1152]{3,2,1,0:T(8,128)(2,1)} %get-tuple-element.92), channel_id=1, source_target_pairs={{0,16},{1,17},{2,18},{3,19},{4,20},{5,21},{6,22},{7,23},{8,24},{9,... | collective-permute-start | bytes 1327112 | tf_op jit(solution)/shard_map/ppermute | solution.py:295
  360.4 2.4 collective-permute-start.23
  365.2 23.4 %collective-permute-done.24 = bf16[1,2,96,1152]{3,2,1,0:T(8,128)(2,1)} collective-permute-done((bf16[1,2,96,1152]{3,2,1,0:T(8,128)(2,1)}, bf16[1,2,96,1152]{3,2,1,0:T(8,128)(2,1)}, u32[]{:S(2)}, u32[]{:S(2)}) %collective-permute-start.24) | collective-permute-done | bytes 442400 | tf_op jit(solution)/shard_map/ppermute | solution.py:295
  388.6 9.5 %collective-permute-done.23 = bf16[1,2,96,1152]{3,2,1,0:T(8,128)(2,1)} collective-permute-done((bf16[1,2,96,1152]{3,2,1,0:T(8,128)(2,1)}, bf16[1,2,96,1152]{3,2,1,0:T(8,128)(2,1)}, u32[]{:S(2)}, u32[]{:S(2)}) %collective-permute-start.23) | collective-permute-done | bytes 442400 | tf_op jit(solution)/shard_map/ppermute | solution.py:295
  402.7 12.3 %collective-permute-done.27 = bf16[2,96,576]{2,1,0:T(8,128)(2,1)S(1)} collective-permute-done((bf16[2,96,576]{2,1,0:T(8,128)(2,1)S(1)}, bf16[2,96,576]{2,1,0:T(8,128)(2,1)S(1)}, u32[]{:S(2)}, u32[]{:S(2)}) %collective-permute-start.27) | collective-permute-done | bytes 221216 | tf_op jit(solution)/shard_map/ppermute | solution.py:295
  415.0 7.5 %collective-permute-done.26 = bf16[2,96,576]{2,1,0:T(8,128)(2,1)S(1)} collective-permute-done((bf16[2,96,576]{2,1,0:T(8,128)(2,1)S(1)}, bf16[2,96,576]{2,1,0:T(8,128)(2,1)S(1)}, u32[]{:S(2)}, u32[]{:S(2)}) %collective-permute-start.26) | collective-permute-done | bytes 221216 | tf_op jit(solution)/shard_map/ppermute | solution.py:295
  427.3 11.1 %collective-permute-done.19 = bf16[1,128,768]{1,2,0:T(8,128)(2,1)S(1)} collective-permute-done((bf16[1,128,768]{1,2,0:T(8,128)(2,1)S(1)}, bf16[1,128,768]{1,2,0:T(8,128)(2,1)S(1)}, u32[]{:S(2)}, u32[]{:S(2)}) %collective-permute-start.19) | collective-permute-done | bytes 196640 | tf_op jit(solution)/shard_map/ppermute | solution.py:295
  439.9 7.7 %fusion.34 = (f32[1152]{0:T(1024)S(1)}, f32[128]{0:T(128)S(1)}, f32[128,1152]{1,0:T(8,128)}) fusion(bf16[128,1152]{1,0:T(8,128)(2,1)S(1)} %copy-done.12, f32[128]{0:T(128)S(1)} %copy-done.51, f32[1152]{0:T(1024)S(1)} %copy-done.41, bf16[576,1920]{1,0:T(8,128)(2,1)} %copy-done.15, bf16[576,1920]{1,0:T(8,128)(2,1)} %constant_dynamic-update-slice_fusion, ...), kind=kOutput, calls=%fused_computation.69 | convolution fusion | flops 588643072 | bytes 5810177 | tf_op jit(solution)/shard_map/th,dh->td/dot_general | solution.py:531
  448.9 88.4 %exchange.1 = (bf16[32,128,256]{2,1,0:T(8,128)(2,1)S(1)}, f32[32,8,1152]{2,1,0:T(8,128)S(1)}) custom-call(bf16[16,128,256]{2,1,0:T(8,128)(2,1)S(1)} %fusion.17.blocks, f32[8,1152]{1,0:T(8,128)S(1)} %select_maximum_fusion.small), custom_call_target="tpu_custom_call" | custom-call | tf_op jit(solution)/shard_map/exchange/pallas_call | solution.py:253
  538.7 4.0 fusion.20
  546.0 2.1 fusion.33
  548.1 5.7 %fusion.18 = f32[576,72]{0,1:T(8,128)} fusion(bf16[4096,576]{0,1:T(8,128)(2,1)} %all-gather.8.cloned.1.call-done, bf16[4096,256]{1,0:T(8,128)(2,1)} %bitcast.90), kind=kOutput, calls=%fused_computation.49 | convolution fusion | flops 339738624 | bytes 5933056 | tf_op jit(solution)/shard_map/th,td->hd/dot_general | solution.py:553
  (261 shorter events, 102.4 us)
Async XLA Ops:
  8.0 183.7 %copy-start = (bf16[1536,1152]{1,0:T(8,128)(2,1)S(1)}, bf16[1536,1152]{1,0:T(8,128)(2,1)}, u32[]{:S(2)}) copy-start(bf16[1536,1152]{1,0:T(8,128)(2,1)} %param.19) | copy-start | bytes 10616836
  8.0 139.0 %all-gather.4.cloned.1.call-start = ((), (), s32[]{:S(2)}) async-start(), calls=%async_computation | async-start | bytes 6488064 | tf_op jit(solution)/shard_map/all_gather | solution.py:434
  16.9 25.6 %collective-permute-start.1 = (bf16[288,1920]{1,0:T(8,128)(2,1)}, bf16[288,1920]{1,0:T(8,128)(2,1)}, u32[]{:S(2)}, u32[]{:S(2)}) collective-permute-start(bf16[288,1920]{1,0:T(8,128)(2,1)} %constant_dynamic-slice_fusion.18), channel_id=1, source_target_pairs={{0,1},{1,0},{2,3},{3,2},{4,5},{5,4},{6,7},{7,6},{8,9},{9,8},{10,11... | collective-permute-start | bytes 3317768 | tf_op jit(solution)/shard_map/ppermute | solution.py:295
  18.3 27.4 %collective-permute-start = (bf16[2,576]{1,0:T(2,128)(2,1)}, bf16[2,576]{1,0:T(2,128)(2,1)}, u32[]{:S(2)}, u32[]{:S(2)}) collective-permute-start(bf16[2,576]{1,0:T(2,128)(2,1)} %pad_maximum_fusion.12), channel_id=1, source_target_pairs={{0,1},{1,0},{2,3},{3,2},{4,5},{5,4},{6,7},{7,6},{8,9},{9,8},{10,11... | collective-permute-start | bytes 6920 | tf_op jit(solution)/shard_map/ppermute | solution.py:295
  42.5 5.9 %collective-permute-start.2 = (bf16[288,1920]{1,0:T(8,128)(2,1)}, bf16[288,1920]{1,0:T(8,128)(2,1)}, u32[]{:S(2)}, u32[]{:S(2)}) collective-permute-start(bf16[288,1920]{1,0:T(8,128)(2,1)} %collective-permute-done.1), channel_id=1, source_target_pairs={{0,2},{1,3},{2,0},{3,1},{4,6},{5,7},{6,4},{7,5},{8,10},{9,11},{10,... | collective-permute-start | bytes 3317768 | tf_op jit(solution)/shard_map/ppermute | solution.py:295
  63.4 475.3 %all-gather.6.cloned.1.call-start = ((), (), s32[]{:S(2)}) async-start(), calls=%async_computation.1 | async-start | bytes 5013504 | tf_op jit(solution)/shard_map/all_gather | solution.py:538
  65.5 18.3 %collective-permute-start.3 = (bf16[288,1152]{1,0:T(8,128)(2,1)}, bf16[288,1152]{1,0:T(8,128)(2,1)}, u32[]{:S(2)}, u32[]{:S(2)}) collective-permute-start(bf16[288,1152]{1,0:T(8,128)(2,1)} %constant_dynamic-slice_fusion.17), channel_id=1, source_target_pairs={{0,1},{1,0},{2,3},{3,2},{4,5},{5,4},{6,7},{7,6},{8,9},{9,8},{10,11... | collective-permute-start | bytes 1990664 | tf_op jit(solution)/shard_map/ppermute | solution.py:295
  83.7 14.0 %collective-permute-start.4 = (bf16[288,1152]{1,0:T(8,128)(2,1)}, bf16[288,1152]{1,0:T(8,128)(2,1)}, u32[]{:S(2)}, u32[]{:S(2)}) collective-permute-start(bf16[288,1152]{1,0:T(8,128)(2,1)} %collective-permute-done.3), channel_id=1, source_target_pairs={{0,2},{1,3},{2,0},{3,1},{4,6},{5,7},{6,4},{7,5},{8,10},{9,11},{10,... | collective-permute-start | bytes 1990664 | tf_op jit(solution)/shard_map/ppermute | solution.py:295
  89.3 95.0 %collective-permute-start.7 = (bf16[576,1536]{1,0:T(8,128)(2,1)}, bf16[576,1536]{1,0:T(8,128)(2,1)}, u32[]{:S(2)}, u32[]{:S(2)}) collective-permute-start(bf16[576,1536]{1,0:T(8,128)(2,1)} %pad_maximum_fusion.1), channel_id=1, source_target_pairs={{0,1},{1,0},{2,3},{3,2},{4,5},{5,4},{6,7},{7,6},{8,9},{9,8},{10,11... | collective-permute-start | bytes 5308424 | tf_op jit(solution)/shard_map/ppermute | solution.py:295
  89.5 81.0 %collective-permute-start.10 = (bf16[128,1152]{1,0:T(8,128)(2,1)}, bf16[128,1152]{1,0:T(8,128)(2,1)}, u32[]{:S(2)}, u32[]{:S(2)}) collective-permute-start(bf16[128,1152]{1,0:T(8,128)(2,1)} %param.23), channel_id=1, source_target_pairs={{0,1},{1,0},{2,3},{3,2},{4,5},{5,4},{6,7},{7,6},{8,9},{9,8},{10,11... | collective-permute-start | bytes 884744 | tf_op jit(solution)/shard_map/ppermute | solution.py:295
  97.5 71.0 %collective-permute-start.20 = (bf16[128,576]{0,1:T(8,128)(2,1)}, bf16[128,576]{0,1:T(8,128)(2,1)}, u32[]{:S(2)}, u32[]{:S(2)}) collective-permute-start(bf16[128,576]{0,1:T(8,128)(2,1)} %get-tuple-element.115), channel_id=1, source_target_pairs={{0,1},{1,0},{2,3},{3,2},{4,5},{5,4},{6,7},{7,6},{8,9},{9,8},{10,11... | collective-permute-start | bytes 442376 | tf_op jit(solution)/shard_map/ppermute | solution.py:295
  167.3 8.7 %collective-permute-start.5 = (bf16[128,1152]{1,0:T(8,128)(2,1)}, bf16[128,1152]{1,0:T(8,128)(2,1)}, u32[]{:S(2)}, u32[]{:S(2)}) collective-permute-start(bf16[128,1152]{1,0:T(8,128)(2,1)} %multiply_convert_fusion.3), channel_id=1, source_target_pairs={{0,1},{1,0},{2,3},{3,2},{4,5},{5,4},{6,7},{7,6},{8,9},{9,8},{10,11... | collective-permute-start | bytes 884744 | tf_op jit(solution)/shard_map/ppermute | solution.py:295
  170.3 377.8 %all-gather.8.cloned.1.call-start = ((), (), s32[]{:S(2)}) async-start(), calls=%async_computation.2 | async-start | bytes 5013504 | tf_op jit(solution)/shard_map/all_gather | solution.py:539
  172.5 9.9 %collective-permute-start.11 = (bf16[256,1152]{1,0:T(8,128)(2,1)}, bf16[256,1152]{1,0:T(8,128)(2,1)}, u32[]{:S(2)}, u32[]{:S(2)}) collective-permute-start(bf16[256,1152]{1,0:T(8,128)(2,1)} %pad_maximum_fusion.7), channel_id=1, source_target_pairs={{0,2},{1,3},{2,0},{3,1},{4,6},{5,7},{6,4},{7,5},{8,10},{9,11},{10,... | collective-permute-start | bytes 1769480 | tf_op jit(solution)/shard_map/ppermute | solution.py:295
  177.9 6.4 %collective-permute-start.6 = (bf16[256,1152]{1,0:T(8,128)(2,1)}, bf16[256,1152]{1,0:T(8,128)(2,1)}, u32[]{:S(2)}, u32[]{:S(2)}) collective-permute-start(bf16[256,1152]{1,0:T(8,128)(2,1)} %pad_maximum_fusion.6), channel_id=1, source_target_pairs={{0,2},{1,3},{2,0},{3,1},{4,6},{5,7},{6,4},{7,5},{8,10},{9,11},{10,... | collective-permute-start | bytes 1769480 | tf_op jit(solution)/shard_map/ppermute | solution.py:295
  199.7 3.3 collective-permute-start.12
  202.4 3.6 collective-permute-start.8
  204.7 8.8 %collective-permute-start.13 = (bf16[128,1152]{1,0:T(8,128)(2,1)S(1)}, bf16[128,1152]{1,0:T(8,128)(2,1)S(1)}, u32[]{:S(2)}, u32[]{:S(2)}) collective-permute-start(bf16[128,1152]{1,0:T(8,128)(2,1)S(1)} %slice.237), channel_id=1, source_target_pairs={{0,1},{1,0},{2,3},{3,2},{4,5},{5,4},{6,7},{7,6},{8,9},{9,8},{10,11... | collective-permute-start | bytes 884744 | tf_op jit(solution)/shard_map/ppermute | solution.py:295
  207.2 14.8 %copy-start.22 = (bf16[576,1152]{1,0:T(8,128)(2,1)S(1)}, bf16[576,1152]{1,0:T(8,128)(2,1)}, u32[]{:S(2)}) copy-start(bf16[576,1152]{1,0:T(8,128)(2,1)} %maximum_select_fusion.4) | copy-start | bytes 3981316
  207.2 12.6 %collective-permute-start.9 = (bf16[128,1152]{1,0:T(8,128)(2,1)S(1)}, bf16[128,1152]{1,0:T(8,128)(2,1)S(1)}, u32[]{:S(2)}, u32[]{:S(2)}) collective-permute-start(bf16[128,1152]{1,0:T(8,128)(2,1)S(1)} %slice.238), channel_id=1, source_target_pairs={{0,1},{1,0},{2,3},{3,2},{4,5},{5,4},{6,7},{7,6},{8,9},{9,8},{10,11... | collective-permute-start | bytes 884744 | tf_op jit(solution)/shard_map/ppermute | solution.py:295
  252.6 62.1 %collective-permute-start.14 = (bf16[8,2,128,768]{3,2,0,1:T(8,128)(2,1)}, bf16[8,2,128,768]{3,2,0,1:T(8,128)(2,1)}, u32[]{:S(2)}, u32[]{:S(2)}) collective-permute-start(bf16[8,2,128,768]{3,2,0,1:T(8,128)(2,1)} %bitcast.87), channel_id=1, source_target_pairs={{0,2},{1,3},{2,0},{3,1},{4,6},{5,7},{6,4},{7,5},{8,10},{9,11},{10,... | collective-permute-start | bytes 9437192 | tf_op jit(solution)/shard_map/ppermute | solution.py:295
  257.1 21.6 %collective-permute-start.28 = (bf16[4,144,768]{2,1,0:T(8,128)(2,1)}, bf16[4,144,768]{2,1,0:T(8,128)(2,1)}, u32[]{:S(2)}, u32[]{:S(2)}) collective-permute-start(bf16[4,144,768]{2,1,0:T(8,128)(2,1)} %dynamic-slice_bitcast_fusion.2), channel_id=1, source_target_pairs={{0,4},{1,5},{2,6},{3,7},{4,0},{5,1},{6,2},{7,3},{8,12},{9,13},{10,... | collective-permute-start | bytes 2654216 | tf_op jit(solution)/shard_map/ppermute | solution.py:295
  257.1 5.6 %collective-permute-start.21 = (bf16[128,576]{0,1:T(8,128)(2,1)S(1)}, bf16[128,576]{0,1:T(8,128)(2,1)S(1)}, u32[]{:S(2)}, u32[]{:S(2)}) collective-permute-start(bf16[128,576]{0,1:T(8,128)(2,1)S(1)} %get-tuple-element.111), channel_id=1, source_target_pairs={{0,1},{1,0},{2,3},{3,2},{4,5},{5,4},{6,7},{7,6},{8,9},{9,8},{10,11... | collective-permute-start | bytes 442376 | tf_op jit(solution)/shard_map/ppermute | solution.py:295
  269.0 69.6 %collective-permute-start.22 = (bf16[4,2,96,1152]{3,2,1,0:T(8,128)(2,1)}, bf16[4,2,96,1152]{3,2,1,0:T(8,128)(2,1)}, u32[]{:S(2)}, u32[]{:S(2)}) collective-permute-start(bf16[4,2,96,1152]{3,2,1,0:T(8,128)(2,1)} %dynamic-slice_bitcast_fusion), channel_id=1, source_target_pairs={{0,4},{1,5},{2,6},{3,7},{4,0},{5,1},{6,2},{7,3},{8,12},{9,13},{10,... | collective-permute-start | bytes 5308424 | tf_op jit(solution)/shard_map/ppermute | solution.py:295
  272.3 42.4 %copy-start.5 = (bf16[8,1,2,128,768]{4,3,2,1,0:T(8,128)(2,1)S(1)}, bf16[8,1,2,128,768]{4,3,2,1,0:T(8,128)(2,1)}, u32[]{:S(2)}) copy-start(bf16[8,1,2,128,768]{4,3,2,1,0:T(8,128)(2,1)} %get-tuple-element.81) | copy-start | bytes 9437188
  280.3 34.4 %copy-start.9 = (bf16[4,144,768]{2,1,0:T(8,128)(2,1)}, bf16[4,144,768]{2,1,0:T(8,128)(2,1)S(1)}, u32[]{:S(2)}) copy-start(bf16[4,144,768]{2,1,0:T(8,128)(2,1)S(1)} %fusion.7) | copy-start | bytes 2654212
  281.2 50.1 %collective-permute-start.31 = (bf16[1,144,768]{2,1,0:T(8,128)(2,1)}, bf16[1,144,768]{2,1,0:T(8,128)(2,1)}, u32[]{:S(2)}, u32[]{:S(2)}) collective-permute-start(bf16[1,144,768]{2,1,0:T(8,128)(2,1)} %get-tuple-element.98), channel_id=1, source_target_pairs={{0,24},{1,25},{2,26},{3,27},{4,28},{5,29},{6,30},{7,31},{8,0},{9,1... | collective-permute-start | bytes 663560 | tf_op jit(solution)/shard_map/ppermute | solution.py:295
  281.2 50.1 %collective-permute-start.30 = (bf16[1,144,768]{2,1,0:T(8,128)(2,1)}, bf16[1,144,768]{2,1,0:T(8,128)(2,1)}, u32[]{:S(2)}, u32[]{:S(2)}) collective-permute-start(bf16[1,144,768]{2,1,0:T(8,128)(2,1)} %get-tuple-element.99), channel_id=1, source_target_pairs={{0,16},{1,17},{2,18},{3,19},{4,20},{5,21},{6,22},{7,23},{8,24},{9,... | collective-permute-start | bytes 663560 | tf_op jit(solution)/shard_map/ppermute | solution.py:295
  312.3 22.6 %collective-permute-start.29 = (bf16[1,144,768]{2,1,0:T(8,128)(2,1)}, bf16[1,144,768]{2,1,0:T(8,128)(2,1)}, u32[]{:S(2)}, u32[]{:S(2)}) collective-permute-start(bf16[1,144,768]{2,1,0:T(8,128)(2,1)} %get-tuple-element.97), channel_id=1, source_target_pairs={{0,8},{1,9},{2,10},{3,11},{4,12},{5,13},{6,14},{7,15},{8,16},{9,17... | collective-permute-start | bytes 663560 | tf_op jit(solution)/shard_map/ppermute | solution.py:295
  320.5 42.2 %collective-permute-start.15 = (bf16[8,128,768]{2,1,0:T(8,128)(2,1)}, bf16[8,128,768]{2,1,0:T(8,128)(2,1)}, u32[]{:S(2)}, u32[]{:S(2)}) collective-permute-start(bf16[8,128,768]{2,1,0:T(8,128)(2,1)} %dynamic-slice_bitcast_fusion.1), channel_id=1, source_target_pairs={{0,1},{1,0},{2,3},{3,2},{4,5},{5,4},{6,7},{7,6},{8,9},{9,8},{10,11... | collective-permute-start | bytes 4718600 | tf_op jit(solution)/shard_map/ppermute | solution.py:295
  336.4 1.5 collective-permute-start.32
  338.6 24.1 %copy-start.4 = (bf16[8,2,128,768]{3,2,0,1:T(8,128)(2,1)S(1)}, bf16[8,2,128,768]{3,2,0,1:T(8,128)(2,1)}, u32[]{:S(2)}) copy-start(bf16[8,2,128,768]{3,2,0,1:T(8,128)(2,1)} %copy-done.3) | copy-start | bytes 9437188
  340.7 23.9 %copy-start.6 = (bf16[4,2,96,1152]{3,2,1,0:T(8,128)(2,1)}, bf16[4,2,96,1152]{3,2,1,0:T(8,128)(2,1)S(1)}, u32[]{:S(2)}) copy-start(bf16[4,2,96,1152]{3,2,1,0:T(8,128)(2,1)S(1)} %fusion.1) | copy-start | bytes 5308420
  341.9 23.3 %collective-permute-start.25 = (bf16[1,2,96,1152]{3,2,1,0:T(8,128)(2,1)}, bf16[1,2,96,1152]{3,2,1,0:T(8,128)(2,1)}, u32[]{:S(2)}, u32[]{:S(2)}) collective-permute-start(bf16[1,2,96,1152]{3,2,1,0:T(8,128)(2,1)} %get-tuple-element.91), channel_id=1, source_target_pairs={{0,24},{1,25},{2,26},{3,27},{4,28},{5,29},{6,30},{7,31},{8,0},{9,1... | collective-permute-start | bytes 1327112 | tf_op jit(solution)/shard_map/ppermute | solution.py:295
  341.9 46.7 %collective-permute-start.24 = (bf16[1,2,96,1152]{3,2,1,0:T(8,128)(2,1)}, bf16[1,2,96,1152]{3,2,1,0:T(8,128)(2,1)}, u32[]{:S(2)}, u32[]{:S(2)}) collective-permute-start(bf16[1,2,96,1152]{3,2,1,0:T(8,128)(2,1)} %get-tuple-element.92), channel_id=1, source_target_pairs={{0,16},{1,17},{2,18},{3,19},{4,20},{5,21},{6,22},{7,23},{8,24},{9,... | collective-permute-start | bytes 1327112 | tf_op jit(solution)/shard_map/ppermute | solution.py:295
  360.4 37.7 %collective-permute-start.23 = (bf16[1,2,96,1152]{3,2,1,0:T(8,128)(2,1)}, bf16[1,2,96,1152]{3,2,1,0:T(8,128)(2,1)}, u32[]{:S(2)}, u32[]{:S(2)}) collective-permute-start(bf16[1,2,96,1152]{3,2,1,0:T(8,128)(2,1)} %get-tuple-element.90), channel_id=1, source_target_pairs={{0,8},{1,9},{2,10},{3,11},{4,12},{5,13},{6,14},{7,15},{8,16},{9,17... | collective-permute-start | bytes 1327112 | tf_op jit(solution)/shard_map/ppermute | solution.py:295
  364.7 37.2 %copy-start.29 = (f32[72,768]{1,0:T(8,128)S(1)}, f32[72,768]{1,0:T(8,128)}, u32[]{:S(2)}) copy-start(f32[72,768]{1,0:T(8,128)} %dynamic-slice_bitcast_fusion.3) | copy-start | bytes 663556
  364.7 37.2 %copy-start.30 = (f32[72,768]{1,0:T(8,128)S(1)}, f32[72,768]{1,0:T(8,128)}, u32[]{:S(2)}) copy-start(f32[72,768]{1,0:T(8,128)} %convert_element_type.277) | copy-start | bytes 663556
  365.1 57.9 %collective-permute-start.16 = (bf16[4,128,768]{1,2,0:T(8,128)(2,1)S(1)}, bf16[4,128,768]{1,2,0:T(8,128)(2,1)}, u32[]{:S(2)}, u32[]{:S(2)}) collective-permute-start(bf16[4,128,768]{1,2,0:T(8,128)(2,1)S(1)} %bitcast.110), channel_id=1, source_target_pairs={{0,4},{1,5},{2,6},{3,7},{4,0},{5,1},{6,2},{7,3},{8,12},{9,13},{10,... | collective-permute-start | bytes 2359304 | tf_op jit(solution)/shard_map/ppermute | solution.py:295
  399.9 15.1 %collective-permute-start.27 = (bf16[2,96,576]{2,1,0:T(8,128)(2,1)S(1)}, bf16[2,96,576]{2,1,0:T(8,128)(2,1)S(1)}, u32[]{:S(2)}, u32[]{:S(2)}) collective-permute-start(bf16[2,96,576]{2,1,0:T(8,128)(2,1)S(1)} %get-tuple-element.109), channel_id=1, source_target_pairs={{0,1},{1,17},{2,9},{3,25},{4,0},{5,16},{6,8},{7,24},{8,3},{9,19},{... | collective-permute-start | bytes 663560 | tf_op jit(solution)/shard_map/ppermute | solution.py:295
  400.0 22.6 %collective-permute-start.26 = (bf16[2,96,576]{2,1,0:T(8,128)(2,1)S(1)}, bf16[2,96,576]{2,1,0:T(8,128)(2,1)S(1)}, u32[]{:S(2)}, u32[]{:S(2)}) collective-permute-start(bf16[2,96,576]{2,1,0:T(8,128)(2,1)S(1)} %get-tuple-element.108), channel_id=1, source_target_pairs={{0,0},{1,16},{2,8},{3,24},{4,1},{5,17},{6,9},{7,25},{8,2},{9,18},{... | collective-permute-start | bytes 663560 | tf_op jit(solution)/shard_map/ppermute | solution.py:295
  424.4 13.9 %collective-permute-start.19 = (bf16[1,128,768]{1,2,0:T(8,128)(2,1)S(1)}, bf16[1,128,768]{1,2,0:T(8,128)(2,1)S(1)}, u32[]{:S(2)}, u32[]{:S(2)}) collective-permute-start(bf16[1,128,768]{1,2,0:T(8,128)(2,1)S(1)} %get-tuple-element.103), channel_id=1, source_target_pairs={{0,24},{1,25},{2,26},{3,27},{4,28},{5,29},{6,30},{7,31},{8,0},{9,1... | collective-permute-start | bytes 589832 | tf_op jit(solution)/shard_map/ppermute | solution.py:295
  424.5 13.9 %collective-permute-start.18 = (bf16[1,128,768]{1,2,0:T(8,128)(2,1)S(1)}, bf16[1,128,768]{1,2,0:T(8,128)(2,1)S(1)}, u32[]{:S(2)}, u32[]{:S(2)}) collective-permute-start(bf16[1,128,768]{1,2,0:T(8,128)(2,1)S(1)} %get-tuple-element.104), channel_id=1, source_target_pairs={{0,16},{1,17},{2,18},{3,19},{4,20},{5,21},{6,22},{7,23},{8,24},{9,... | collective-permute-start | bytes 589832 | tf_op jit(solution)/shard_map/ppermute | solution.py:295
  424.6 15.3 %copy-start.12 = (bf16[128,1152]{1,0:T(8,128)(2,1)S(1)}, bf16[128,1152]{1,0:T(8,128)(2,1)}, u32[]{:S(2)}) copy-start(bf16[128,1152]{1,0:T(8,128)(2,1)} %param.12) | copy-start | bytes 884740
  424.6 15.3 %copy-start.27 = (bf16[128,18,64]{0,2,1:T(8,128)(2,1)S(1)}, bf16[128,18,64]{0,2,1:T(8,128)(2,1)}, u32[]{:S(2)}) copy-start(bf16[128,18,64]{0,2,1:T(8,128)(2,1)} %maximum_convert_fusion) | copy-start | bytes 884740
  424.6 15.3 %copy-start.41 = (f32[1152]{0:T(1024)S(1)}, f32[1152]{0:T(1024)}, u32[]{:S(2)}) copy-start(f32[1152]{0:T(1024)} %copy-done.40) | copy-start | bytes 13828
  424.6 15.3 %copy-start.51 = (f32[128]{0:T(128)S(1)}, f32[128]{0:T(128)}, u32[]{:S(2)}) copy-start(f32[128]{0:T(128)} %add_rsqrt_fusion.1) | copy-start | bytes 1540
  424.6 13.7 %collective-permute-start.17 = (bf16[1,128,768]{1,2,0:T(8,128)(2,1)S(1)}, bf16[1,128,768]{1,2,0:T(8,128)(2,1)S(1)}, u32[]{:S(2)}, u32[]{:S(2)}) collective-permute-start(bf16[1,128,768]{1,2,0:T(8,128)(2,1)S(1)} %get-tuple-element.102), channel_id=1, source_target_pairs={{0,8},{1,9},{2,10},{3,11},{4,12},{5,13},{6,14},{7,15},{8,16},{9,17... | collective-permute-start | bytes 589832 | tf_op jit(solution)/shard_map/ppermute | solution.py:295
  (44 other events, 223.4 us)
Sparse Core Ops, SparseCore 0:
  63.5 83.4 all-gather.3
Sparse Core Ops, SparseCore 1:
  170.4 64.5 all-gather.5
  263.7 107.6 all-gather.7
